TPU v7x, 256 devices: a whole 4x4x8 slice. The times are simulated.
256 devices in a mesh: dp: 4 (over y), segment: 2 (over x_hi), tm: 32 (over z, x_lo, core).
Axes of the slice: x: 4 (x_hi: 2, x_lo: 2; x = x_hi * 2 + x_lo), y: 4, z: 8, core: 2. Of those that a mesh axis runs over, the one named last changes fastest.
Arguments:
- inputs: bfloat16 [4, 4096, 1536], P('dp', 'tm'), may hold values from -6 to 6
- lengths: int32 [4], P('dp'), may hold values from 1024 to 4096, as said below
- w_first: bfloat16 [2, 1536, 1536], P('segment'), may hold values from -0.15625 to 0.15625
- kernel: float32 [2, 31, 768], P('segment'), may hold values from -1 to 1
- gain_first: float32 [2, 1536], P('segment'), may hold values from 0.1 to 1.9
- gain_second: float32 [2, 768], P('segment'), may hold values from 0.1 to 1.9
- w_second: bfloat16 [2, 768, 1536], P('segment'), may hold values from -0.21875 to 0.21875
- grad_output: bfloat16 [4, 4096, 1536], P('dp', 'tm'), may hold values from -6 to 6
Outputs:
- segment_outputs: bfloat16 [2, 4, 4096, 1536], P('segment', 'dp', 'tm')
- segment_grads: bfloat16 [2, 4, 4096, 1536], P('segment', 'dp', 'tm')
- grad_w_first: float32 [2, 1536, 1536], P('segment', ('dp', 'tm'))
- grad_kernel: float32 [2, 31, 768], P('segment', None, ('dp', 'tm'))
- grad_gain_first: float32 [2, 1536], P('segment', ('dp', 'tm'))
- grad_gain_second: float32 [2, 768], P('segment', ('dp', 'tm'))
- grad_w_second: float32 [2, 768, 1536], P('segment', ('dp', 'tm'))
Inputs may be any that keep to these rules, and one draw needn't show every extreme that they name: `lengths`: at least one utterance has all 4096 frames valid.
All inputs are finite; a program needn't handle non-finite values.
Results may differ from a plain program's by a relative error of at most 0.04.
Values may be sent and summed in bfloat16 or wider, within the bound.
A program may use at most 128 MiB of HBM per device.

v0:
```python
import jax
import jax.numpy as jnp
from jax import lax
from jax.sharding import PartitionSpec as P

EPS = 1e-05


def extended(shard, sides, width):
    for axis, dim in sides:
        size, length = (lax.axis_size(axis), shard.shape[dim])
        up = [(i, (i + 1) % size) for i in range(size - 1)]
        down = [(j, i) for i, j in up]
        last = lax.slice_in_dim(shard, length - width, length, axis=dim)
        first = lax.slice_in_dim(shard, 0, width, axis=dim)
        before = lax.ppermute(last, axis, up)
        after = lax.ppermute(first, axis, down)
        shard = jnp.concatenate([before, shard, after], axis=dim)
    return shard


def passed_along(shard, axis, by):
    length = lax.axis_size(axis)
    pairs = [(i, i + by) for i in range(length) if 0 <= i + by < length]
    return lax.ppermute(shard, axis, pairs)


def normalize(values, gain):
    mean = jnp.mean(values, axis=-1, keepdims=True)
    centred = values - mean
    spread = jnp.mean(centred * centred, axis=-1, keepdims=True)
    return centred * lax.rsqrt(spread + EPS) * gain


def swish_norm(values, gain):
    normal = normalize(values, gain)
    return normal * jax.nn.sigmoid(normal)


def depthwise(padded, kern):
    count = padded.shape[0] - kern.shape[0] + 1
    total = jnp.zeros((count, padded.shape[1]), jnp.float32)
    for shift_k in range(kern.shape[0]):
        total = total + kern[shift_k] * padded[shift_k : shift_k + count]
    return total


def section_forward(current, chosen, maskf, w_one, kern, gain_one, gain_two, w_two):
    half = kern.shape[0] // 2
    count = current.shape[0]
    width = w_one.shape[1] // 2
    model = current.shape[1]

    def front_work(hidden):
        normed = normalize(hidden.astype(jnp.float32), gain_one).astype(jnp.bfloat16)
        pre = jnp.dot(normed, w_one, preferred_element_type=jnp.float32)
        gated = (pre[:, :width] * jax.nn.sigmoid(pre[:, width:]) * maskf).astype(jnp.bfloat16)
        return (normed, pre, gated)

    def front_skip(hidden):
        return (
            jnp.zeros((count, model), jnp.bfloat16),
            jnp.zeros((count, 2 * width), jnp.float32),
            jnp.zeros((count, width), jnp.bfloat16),
        )

    normed, pre, gated = lax.cond(chosen, front_work, front_skip, current)
    padded = extended(gated, (("tm", 0),), half).astype(jnp.float32)

    def tail_work(operands):
        hidden, padded_in = operands
        conv = depthwise(padded_in, kern)
        act = swish_norm(conv, gain_two).astype(jnp.bfloat16)
        out = jnp.dot(act, w_two, preferred_element_type=jnp.float32)
        result = (hidden.astype(jnp.float32) + maskf * out).astype(jnp.bfloat16)
        return (result, conv, act)

    def tail_skip(operands):
        return (
            jnp.zeros((count, model), jnp.bfloat16),
            jnp.zeros((count, width), jnp.float32),
            jnp.zeros((count, width), jnp.bfloat16),
        )

    result, conv, act = lax.cond(chosen, tail_work, tail_skip, (current, padded))
    return (result, (normed, pre, padded, conv, act))


def section_backward(hidden, chosen, maskf, stash, w_one, kern, gain_one, gain_two, w_two, grad_in):
    normed, pre, padded, conv, act = stash
    half = kern.shape[0] // 2
    count = hidden.shape[0]
    model = hidden.shape[1]
    width = w_one.shape[1] // 2
    taps = kern.shape[0]

    def upper_work(operands):
        grad_val, conv_in, act_in = operands
        upstream = grad_val.astype(jnp.float32)
        d_out = (upstream * maskf).astype(jnp.bfloat16)
        grad_two = jnp.dot(act_in.T, d_out, preferred_element_type=jnp.float32)
        d_act = jnp.dot(d_out, w_two.T, preferred_element_type=jnp.float32)
        _, pull_tail = jax.vjp(swish_norm, conv_in, gain_two)
        d_conv, grad_gain_two = pull_tail(d_act)
        return (upstream, grad_two, d_conv, grad_gain_two)

    def upper_skip(operands):
        return (
            jnp.zeros((count, model), jnp.float32),
            jnp.zeros((width, model), jnp.float32),
            jnp.zeros((count, width), jnp.float32),
            jnp.zeros((width,), jnp.float32),
        )

    upstream, grad_two, d_conv, grad_gain_two = lax.cond(
        chosen, upper_work, upper_skip, (grad_in, conv, act)
    )
    d_padded = extended(d_conv.astype(jnp.bfloat16), (("tm", 0),), half).astype(d_conv.dtype)

    def lower_work(operands):
        hidden_in, normed_in, pre_in, padded_in, d_conv_in, d_padded_in, upstream_in = operands
        grad_kern = jnp.stack(
            [jnp.sum(padded_in[k : k + count] * d_conv_in, axis=0) for k in range(taps)]
        )
        d_gated = depthwise(d_padded_in, kern[::-1]) * maskf
        first = pre_in[:, :width]
        sig = jax.nn.sigmoid(pre_in[:, width:])
        d_pre = jnp.concatenate(
            [d_gated * sig, d_gated * first * sig * (1.0 - sig)], axis=1
        ).astype(jnp.bfloat16)
        grad_one = jnp.dot(normed_in.T, d_pre, preferred_element_type=jnp.float32)
        d_normed = jnp.dot(d_pre, w_one.T, preferred_element_type=jnp.float32)
        _, pull_front = jax.vjp(normalize, hidden_in.astype(jnp.float32), gain_one)
        d_hidden, grad_gain_one = pull_front(d_normed)
        grad_hidden = (upstream_in + d_hidden).astype(jnp.bfloat16)
        return (grad_hidden, grad_one, grad_kern, grad_gain_one)

    def lower_skip(operands):
        return (
            jnp.zeros((count, model), jnp.bfloat16),
            jnp.zeros((model, 2 * width), jnp.float32),
            jnp.zeros((taps, width), jnp.float32),
            jnp.zeros((model,), jnp.float32),
        )

    grad_hidden, grad_one, grad_kern, grad_gain_one = lax.cond(
        chosen, lower_work, lower_skip, (hidden, normed, pre, padded, d_conv, d_padded, upstream)
    )
    return (grad_hidden, (grad_one, grad_kern, grad_gain_one, grad_gain_two, grad_two))


def pick_tree(chosen, fresh, older):
    return jax.tree.map(lambda new_val, old_val: jnp.where(chosen, new_val, old_val), fresh, older)


def per_device(inputs, lengths, w_first, kernel, gain_first, gain_second, w_second, grad_output):
    sections = lax.axis_size("segment")
    here = lax.axis_index("segment")
    n_data = lax.axis_size("dp")
    n_time = lax.axis_size("tm")
    count = inputs.shape[1]
    frame_ids = lax.axis_index("tm") * count + jnp.arange(count, dtype=jnp.int32)
    maskf = (frame_ids < lengths[0]).astype(jnp.float32)[:, None]
    w_one = w_first[0]
    kern = kernel[0]
    gain_one = gain_first[0]
    gain_two = gain_second[0]
    w_two = w_second[0]
    model = w_one.shape[0]
    width = w_one.shape[1] // 2
    taps = kern.shape[0]
    groups = n_data * n_time
    current = inputs[0]
    kept_hidden = current
    kept_result = None
    kept_stash = None
    for step in range(sections):
        chosen = here == step
        result, stash = section_forward(
            current, chosen, maskf, w_one, kern, gain_one, gain_two, w_two
        )
        if step == 0:
            kept_result = result
            kept_stash = stash
        else:
            kept_hidden = jnp.where(chosen, current, kept_hidden)
            kept_result = jnp.where(chosen, result, kept_result)
            kept_stash = pick_tree(chosen, stash, kept_stash)
        if step + 1 < sections:
            current = passed_along(result, "segment", 1)
    upstream = grad_output[0]
    kept_grad = None
    kept_weights = None
    for step in range(sections):
        target = sections - 1 - step
        chosen = here == target
        grad_hidden, weight_grads = section_backward(
            kept_hidden, chosen, maskf, kept_stash, w_one, kern, gain_one, gain_two, w_two, upstream
        )
        if step == 0:
            kept_grad = grad_hidden
            kept_weights = weight_grads
        else:
            kept_grad = jnp.where(chosen, grad_hidden, kept_grad)
            kept_weights = pick_tree(chosen, weight_grads, kept_weights)
        if step + 1 < sections:
            upstream = passed_along(grad_hidden, "segment", -1)
    grad_one, grad_kern, grad_gain_one, grad_gain_two, grad_two = kept_weights
    term_one = grad_one.astype(jnp.bfloat16).reshape(1, n_data, n_time, model // groups, 2 * width)
    term_kern = grad_kern.astype(jnp.bfloat16).reshape(1, taps, n_data, n_time, width // groups)
    term_gain_one = grad_gain_one.astype(jnp.bfloat16).reshape(1, n_data, n_time, model // groups)
    term_gain_two = grad_gain_two.astype(jnp.bfloat16).reshape(1, n_data, n_time, width // groups)
    term_two = grad_two.astype(jnp.bfloat16).reshape(1, n_data, n_time, width // groups, model)
    shares = (
        lax.psum_scatter(term_one, "tm", scatter_dimension=2, tiled=True).astype(jnp.float32),
        lax.psum_scatter(term_kern, "tm", scatter_dimension=3, tiled=True).astype(jnp.float32),
        lax.psum_scatter(term_gain_one, "tm", scatter_dimension=2, tiled=True).astype(jnp.float32),
        lax.psum_scatter(term_gain_two, "tm", scatter_dimension=2, tiled=True).astype(jnp.float32),
        lax.psum_scatter(term_two, "tm", scatter_dimension=2, tiled=True).astype(jnp.float32),
    )
    summed = (
        lax.psum_scatter(
            shares[0].astype(jnp.bfloat16), "dp", scatter_dimension=1, tiled=True
        ).astype(jnp.float32),
        lax.psum_scatter(
            shares[1].astype(jnp.bfloat16), "dp", scatter_dimension=2, tiled=True
        ).astype(jnp.float32),
        lax.psum_scatter(
            shares[2].astype(jnp.bfloat16), "dp", scatter_dimension=1, tiled=True
        ).astype(jnp.float32),
        lax.psum_scatter(
            shares[3].astype(jnp.bfloat16), "dp", scatter_dimension=1, tiled=True
        ).astype(jnp.float32),
        lax.psum_scatter(
            shares[4].astype(jnp.bfloat16), "dp", scatter_dimension=1, tiled=True
        ).astype(jnp.float32),
    )
    return (
        kept_result[None, None],
        kept_grad[None, None],
        summed[0].reshape(1, model // groups, 2 * width),
        summed[1].reshape(1, taps, width // groups),
        summed[2].reshape(1, model // groups),
        summed[3].reshape(1, width // groups),
        summed[4].reshape(1, width // groups, model),
    )


def solution(mesh):
    in_specs = (
        P("dp", "tm", None),
        P("dp"),
        P("segment", None, None),
        P("segment", None, None),
        P("segment", None),
        P("segment", None),
        P("segment", None, None),
        P("dp", "tm", None),
    )
    out_specs = (
        P("segment", "dp", "tm", None),
        P("segment", "dp", "tm", None),
        P("segment", ("dp", "tm"), None),
        P("segment", None, ("dp", "tm")),
        P("segment", ("dp", "tm")),
        P("segment", ("dp", "tm")),
        P("segment", ("dp", "tm"), None),
    )
    return jax.shard_map(
        per_device, mesh=mesh, in_specs=in_specs, out_specs=out_specs, check_vma=False
    )
```

profile of v0, /device:TPU:1, one launch (start us, length us, event | category | flops | bytes accessed | tf_op | source)
XLA Modules:
  0.0 465.1 jit_solution(10157894366309918691)
XLA Ops:
  7.9 10.7 %conditional.8 = (bf16[128,1536]{1,0:T(8,128)(2,1)}, f32[128,1536]{1,0:T(8,128)}, bf16[128,768]{1,0:T(8,128)(2,1)S(1)}) conditional(s32[]{:T(128)} %convert_element_type.136, () %tuple.74, (bf16[128,1536]{1,0:T(8,128)(2,1)}, f32[1,1536]{1,0:T(1,128)}, bf16[1536,1536]{1,0:T(8,128)(2,1)}, f32[128,1]{0,1:T(1,128)S(1)}) %tuple.319), branch_computations={%region_0.0_spmd, %region_1.0_spmd} | conditional | flops 606732416 | bytes 8477724 | solution.py:67
  7.9 1.3 convert_reduce_fusion
  9.2 1.2 fusion.2
  11.2 2.0 fusion.4
  13.2 4.2 fusion.72
  17.4 1.2 fusion.10
  18.7 4.5 collective-permute-start
  23.2 1.9 collective-permute-start.1
  25.8 2.6 collective-permute-done.1
  28.9 10.3 %conditional.9 = (bf16[128,1536]{1,0:T(8,128)(2,1)}, f32[128,768]{1,0:T(8,128)}, bf16[128,768]{1,0:T(8,128)(2,1)}) conditional(s32[]{:T(128)} %convert_element_type.136, () %tuple.73, (bf16[128,1536]{1,0:T(8,128)(2,1)}, f32[128,1]{0,1:T(1,128)S(1)}, f32[31,768]{1,0:T(8,128)}, f32[158,768]{1,0:T(8,128)S(1)}, f32[1,768]{1,0:T(1,128)S(1)}, ...), branch_computations={%region_4.0_spmd, %region_5.0_spmd} | conditional | flops 309952640 | bytes 18793556 | solution.py:85
  29.5 1.2 slice_reduce_fusion.29
  30.7 1.4 slice_reduce_fusion.30
  32.2 1.8 fusion.64
  34.0 1.2 multiply_reduce_fusion
  35.2 1.9 multiply_convert_fusion
  37.1 2.2 fusion.12
  39.2 1.3 collective-permute-start.2
  40.5 7.3 %collective-permute-done.2 = bf16[128,1536]{1,0:T(8,128)(2,1)S(1)} collective-permute-done((bf16[128,1536]{1,0:T(8,128)(2,1)}, bf16[128,1536]{1,0:T(8,128)(2,1)S(1)}, u32[]{:S(2)}, u32[]{:S(2)}) %collective-permute-start.2) | collective-permute-done | bytes 393248 | tf_op jit(solution)/shard_map/ppermute | solution.py:25
  47.9 1.8 conditional.10
  49.7 2.1 collective-permute-start.3
  51.8 2.2 collective-permute-start.4
  54.0 1.2 broadcast_select_fusion.2
  55.3 1.1 broadcast_select_fusion
  56.4 1.2 collective-permute-done.4
  57.6 1.5 conditional.11
  59.1 1.2 broadcast_select_fusion.4
  61.3 1.2 conditional.12
  62.6 3.9 collective-permute-start.5
  66.5 1.9 collective-permute-start.6
  68.6 4.8 %collective-permute-done.6 = bf16[15,768]{1,0:T(8,128)(2,1)S(1)} collective-permute-done((bf16[15,768]{1,0:T(8,128)(2,1)S(1)}, bf16[15,768]{1,0:T(8,128)(2,1)S(1)}, u32[]{:S(2)}, u32[]{:S(2)}) %collective-permute-start.6) | collective-permute-done | bytes 23072 | tf_op jit(solution)/shard_map/ppermute | solution.py:17
  73.4 1.2 conditional.13
  74.6 1.3 collective-permute-start.7
  75.9 56.2 %collective-permute-done.7 = bf16[128,1536]{1,0:T(8,128)(2,1)S(1)} collective-permute-done((bf16[128,1536]{1,0:T(8,128)(2,1)S(1)}, bf16[128,1536]{1,0:T(8,128)(2,1)S(1)}, u32[]{:S(2)}, u32[]{:S(2)}) %collective-permute-start.7) | collective-permute-done | bytes 393248 | tf_op jit(solution)/shard_map/ppermute | solution.py:25
  132.2 9.4 %conditional.14 = (f32[128,1536]{1,0:T(8,128)}, bf16[768,1536]{0,1:T(8,128)(2,1)}, f32[128,768]{1,0:T(8,128)S(1)}, bf16[768]{0:T(1024)(128)(2,1)S(1)}) conditional(s32[]{:T(128)} %convert_element_type.136, () %tuple.81, (bf16[128,1536]{1,0:T(8,128)(2,1)S(1)}, f32[128,1]{0,1:T(1,128)}, bf16[128,768]{1,0:T(8,128)(2,1)S(1)}, ...), branch_computations={%region_61.62_spmd, %region_62.68_spmd} | conditional | flops 607813760 | bytes 11240032 | solution.py:115
  133.2 1.0 convert_element_type.117
  134.2 3.6 multiply_reduce_fusion.36
  138.1 3.4 convolution_bitcast_fusion.2
  141.5 3.4 select_convert_fusion.1
  144.9 4.3 copy.45
  149.2 4.9 %reshape.242 = bf16[1,4,32,6,1536]{4,3,2,1,0:T(8,128)(2,1)} reshape(bf16[768,1536]{1,0:T(8,128)(2,1)} %copy.45) | data formatting | bytes 4718592 | tf_op jit(solution)/shard_map/reshape | solution.py:213
  154.1 3.9 copy.46
  158.2 3.0 collective-permute-start.8
  161.1 1.9 collective-permute-start.9
  163.1 4.1 collective-permute-done.9
  167.3 16.7 %conditional.15 = (bf16[128,1536]{1,0:T(8,128)(2,1)}, bf16[1536,1536]{0,1:T(8,128)(2,1)}, bf16[31,768]{1,0:T(8,128)(2,1)S(1)}, bf16[1536]{0:T(1024)(128)(2,1)S(1)}) conditional(s32[]{:T(128)} %convert_element_type.136, () %tuple.80, (f32[31,768]{1,0:T(8,128)}, f32[158,768]{1,0:T(8,128)S(1)}, f32[128,1]{0,1:T(1,128)S(1)}, ...), branch_computations={%region_68.69_spmd, %region_69.106_spmd} | conditional | flops 1228873600 | bytes 43822116 | solution.py:146
  168.7 1.2 slice_reduce_fusion.122
  169.9 1.4 slice_reduce_fusion.123
  171.3 1.1 multiply_convert_fusion.15
  173.6 4.1 fusion.51
  178.1 2.2 add_convert_fusion.1
  180.3 3.6 convolution_bitcast_fusion.3
  183.9 5.0 %select_convert_fusion = bf16[1536,1536]{0,1:T(8,128)(2,1)} fusion(bf16[1536,1536]{0,1:T(8,128)(2,1)} %get-tuple-element.216, bf16[1536,1536]{0,1:T(8,128)(2,1)} %copy-done, pred[]{:T(512)S(6)} %eq.9), kind=kLoop, calls=%fused_computation.321 | loop fusion | flops 2359296 | bytes 14155777 | tf_op jit(solution)/shard_map/convert_element_type | solution.py:209
  188.9 6.6 %copy.35 = bf16[1536,1536]{1,0:T(8,128)(2,1)} copy(bf16[1536,1536]{0,1:T(8,128)(2,1)} %select_convert_fusion) | data formatting | bytes 9437184 | tf_op jit(solution)/shard_map/convert_element_type | solution.py:209
  195.6 8.1 %reshape.230 = bf16[1,4,32,12,1536]{4,3,2,1,0:T(8,128)(2,1)} reshape(bf16[1536,1536]{1,0:T(8,128)(2,1)} %copy.35) | data formatting | bytes 9437184 | tf_op jit(solution)/shard_map/reshape | solution.py:209
  203.7 6.1 %copy.36 = bf16[1,4,32,12,1536]{4,3,1,0,2:T(8,128)(2,1)} copy(bf16[1,4,32,12,1536]{4,3,2,1,0:T(8,128)(2,1)} %reshape.230) | data formatting | bytes 9437184 | tf_op jit(solution)/shard_map/reshape | solution.py:209
  211.6 1.8 select_bitcast_fusion.1
  214.3 104.5 %all-reduce.6 = (bf16[1,31,4,32,6]{1,2,4,0,3:T(4,128)(2,1)S(1)}, bf16[1,4,32,12]{3,1,0,2:T(4,128)(2,1)S(1)}, bf16[1,4,32,6]{3,1,0,2:T(4,128)(2,1)S(1)}) all-reduce(bf16[1,31,4,32,6]{1,2,4,0,3:T(4,128)(2,1)S(1)} %copy.39, bf16[1,4,32,12]{3,1,0,2:T(4,128)(2,1)S(1)} %copy.41, ...), channel_id=4, replica_groups=mesh['dp'=4,'segment'=2,'tm'=32] {'tm'}, use_global_device_ids=true, to_apply=%region_108.109.clone | all-reduce | flops 26112 | bytes 104448
  320.8 13.9 %all-reduce.7 = (bf16[1,31,4,1,6]{1,4,3,2,0:T(8,128)(2,1)S(1)}, bf16[1,4,1,12]{3,2,1,0:T(2,128)(2,1)S(1)}, bf16[1,4,1,6]{3,2,1,0:T(2,128)(2,1)S(1)}) all-reduce(bf16[1,31,4,1,6]{1,4,3,2,0:T(8,128)(2,1)S(1)} %copy.40, bf16[1,4,1,12]{3,2,1,0:T(2,128)(2,1)S(1)} %copy.42, ...), channel_id=5, replica_groups=mesh['dp'=4,'segment'=2,'tm'=32] {'dp'}, use_global_device_ids=true, to_apply=%region_109.110.clone | all-reduce | flops 816 | bytes 3264
  335.3 1.8 select_bitcast_fusion
  337.2 1.1 fusion.61
  338.9 1.1 fusion.63
  340.0 66.3 %reduce-scatter.8.cloned.1.call-done = bf16[1,4,1,12,1536]{4,3,1,0,2:T(8,128)(2,1)} async-done(((bf16[1,4,32,12,1536]{4,3,1,0,2:T(8,128)(2,1)}), bf16[1,4,1,12,1536]{4,3,1,0,2:T(8,128)(2,1)}) %reduce-scatter.8.cloned.1.call-update) | async-done | bytes 147472 | tf_op jit(solution)/shard_map/reduce_scatter | solution.py:215
  406.3 25.5 %reduce-scatter.14.cloned.1.call-done = bf16[1,1,1,6,1536]{4,3,2,0,1:T(8,128)(2,1)} async-done(((bf16[1,4,1,6,1536]{4,3,2,0,1:T(8,128)(2,1)}), bf16[1,1,1,6,1536]{4,3,2,0,1:T(8,128)(2,1)}) %reduce-scatter.14.cloned.1.call-update) | async-done | bytes 18448 | tf_op jit(solution)/shard_map/reduce_scatter | solution.py:234
  433.2 23.8 %reduce-scatter.10.cloned.1.call-done = bf16[1,1,1,12,1536]{4,3,2,0,1:T(8,128)(2,1)} async-done(((bf16[1,4,1,12,1536]{4,3,2,0,1:T(8,128)(2,1)}), bf16[1,1,1,12,1536]{4,3,2,0,1:T(8,128)(2,1)}) %reduce-scatter.10.cloned.1.call-update) | async-done | bytes 36880 | tf_op jit(solution)/shard_map/reduce_scatter | solution.py:222
  (178 shorter events, 22.1 us)
Async XLA Ops:
  7.2 329.9 %reduce-scatter.12.cloned.1.call-start = ((), (), s32[]{:S(2)}) async-start(), calls=%async_computation.6 | async-start | bytes 3244032 | tf_op jit(solution)/shard_map/reduce_scatter | solution.py:219
  7.9 65.5 %copy-start.20 = (f32[128,1]{0,1:T(1,128)}, f32[128,1]{0,1:T(1,128)S(1)}, u32[]{:S(2)}) copy-start(f32[128,1]{0,1:T(1,128)S(1)} %compare_convert_fusion) | copy-start | bytes 1540
  7.9 17.2 %copy-start.18 = (f32[1,31,768]{2,0,1:T(1,128)S(1)}, f32[1,31,768]{2,0,1:T(1,128)}, u32[]{:S(2)}) copy-start(f32[1,31,768]{2,0,1:T(1,128)} %param.27) | copy-start | bytes 285700
  7.9 20.5 %copy-start.4 = (bf16[1,768,1536]{2,1,0:T(8,128)(2,1)S(1)}, bf16[1,768,1536]{2,1,0:T(8,128)(2,1)}, u32[]{:S(2)}) copy-start(bf16[1,768,1536]{2,1,0:T(8,128)(2,1)} %param.30) | copy-start | bytes 7077892
  7.9 20.5 %copy-start.19 = (f32[1,768]{1,0:T(1,128)S(1)}, f32[1,768]{1,0:T(1,128)}, u32[]{:S(2)}) copy-start(f32[1,768]{1,0:T(1,128)} %param.29) | copy-start | bytes 9220
  18.6 9.8 %copy-start.6 = (bf16[128,768]{1,0:T(8,128)(2,1)}, bf16[128,768]{1,0:T(8,128)(2,1)S(1)}, u32[]{:S(2)}) copy-start(bf16[128,768]{1,0:T(8,128)(2,1)S(1)} %get-tuple-element.198) | copy-start | bytes 589828
  18.7 7.1 %collective-permute-start = (bf16[15,768]{1,0:T(8,128)(2,1)S(1)}, bf16[15,768]{1,0:T(8,128)(2,1)S(1)}, u32[]{:S(2)}, u32[]{:S(2)}) collective-permute-start(bf16[15,768]{1,0:T(8,128)(2,1)S(1)} %get-tuple-element.481), channel_id=1, source_target_pairs={{0,1},{1,2},{2,3},{3,4},{4,5},{5,6},{6,7},{7,8},{8,9},{9,10},{10,1... | collective-permute-start | bytes 69128 | tf_op jit(solution)/shard_map/ppermute | solution.py:16
  23.2 5.1 %collective-permute-start.1 = (bf16[15,768]{1,0:T(8,128)(2,1)S(1)}, bf16[15,768]{1,0:T(8,128)(2,1)S(1)}, u32[]{:S(2)}, u32[]{:S(2)}) collective-permute-start(bf16[15,768]{1,0:T(8,128)(2,1)S(1)} %get-tuple-element.482), channel_id=1, source_target_pairs={{1,0},{2,1},{3,2},{4,3},{5,4},{6,5},{7,6},{8,7},{9,8},{10,9},{11,1... | collective-permute-start | bytes 69128 | tf_op jit(solution)/shard_map/ppermute | solution.py:17
  25.8 2.7 copy-start.13
  28.3 0.6 copy-start.15
  28.4 19.5 %copy-start.17 = (f32[1,1536]{1,0:T(1,128)S(1)}, f32[1,1536]{1,0:T(1,128)}, u32[]{:S(2)}) copy-start(f32[1,1536]{1,0:T(1,128)} %param.28) | copy-start | bytes 18436
  32.1 3.0 copy-start.25
  32.1 4.9 %copy-start.2 = (bf16[128,1536]{1,0:T(8,128)(2,1)S(1)}, bf16[128,1536]{1,0:T(8,128)(2,1)}, u32[]{:S(2)}) copy-start(bf16[128,1536]{1,0:T(8,128)(2,1)} %get-tuple-element.113) | copy-start | bytes 1179652 | tf_op jit(solution)/shard_map/cond
  39.2 8.7 %collective-permute-start.2 = (bf16[128,1536]{1,0:T(8,128)(2,1)}, bf16[128,1536]{1,0:T(8,128)(2,1)S(1)}, u32[]{:S(2)}, u32[]{:S(2)}) collective-permute-start(bf16[128,1536]{1,0:T(8,128)(2,1)} %get-tuple-element.199), channel_id=1, source_target_pairs={{0,32},{1,33},{2,34},{3,35},{4,36},{5,37},{6,38},{7,39},{8,40},{9,... | collective-permute-start | bytes 1179656 | tf_op jit(solution)/shard_map/ppermute | solution.py:25
  47.9 7.4 %copy-start.1 = (bf16[1,128,1536]{2,1,0:T(8,128)(2,1)S(1)}, bf16[1,128,1536]{2,1,0:T(8,128)(2,1)}, u32[]{:S(2)}) copy-start(bf16[1,128,1536]{2,1,0:T(8,128)(2,1)} %param.24) | copy-start | bytes 1179652
  49.7 6.7 %collective-permute-start.3 = (bf16[15,768]{1,0:T(8,128)(2,1)S(1)}, bf16[15,768]{1,0:T(8,128)(2,1)S(1)}, u32[]{:S(2)}, u32[]{:S(2)}) collective-permute-start(bf16[15,768]{1,0:T(8,128)(2,1)S(1)} %get-tuple-element.479), channel_id=1, source_target_pairs={{0,1},{1,2},{2,3},{3,4},{4,5},{5,6},{6,7},{7,8},{8,9},{9,10},{10,1... | collective-permute-start | bytes 69128 | tf_op jit(solution)/shard_map/ppermute | solution.py:16
  51.8 5.8 %collective-permute-start.4 = (bf16[15,768]{1,0:T(8,128)(2,1)S(1)}, bf16[15,768]{1,0:T(8,128)(2,1)S(1)}, u32[]{:S(2)}, u32[]{:S(2)}) collective-permute-start(bf16[15,768]{1,0:T(8,128)(2,1)S(1)} %get-tuple-element.480), channel_id=1, source_target_pairs={{1,0},{2,1},{3,2},{4,3},{5,4},{6,5},{7,6},{8,7},{9,8},{10,9},{11,1... | collective-permute-start | bytes 69128 | tf_op jit(solution)/shard_map/ppermute | solution.py:17
  59.1 2.2 copy-start.9
  61.3 7.1 %copy-start.7 = (bf16[128,768]{1,0:T(8,128)(2,1)S(1)}, bf16[128,768]{1,0:T(8,128)(2,1)}, u32[]{:S(2)}) copy-start(bf16[128,768]{1,0:T(8,128)(2,1)} %copy-done.6) | copy-start | bytes 589828
  61.3 7.1 %copy-start.14 = (bf16[15,768]{1,0:T(8,128)(2,1)S(1)}, bf16[15,768]{1,0:T(8,128)(2,1)}, u32[]{:S(2)}) copy-start(bf16[15,768]{1,0:T(8,128)(2,1)} %copy-done.13) | copy-start | bytes 69124
  61.3 7.1 %copy-start.16 = (bf16[15,768]{1,0:T(8,128)(2,1)S(1)}, bf16[15,768]{1,0:T(8,128)(2,1)}, u32[]{:S(2)}) copy-start(bf16[15,768]{1,0:T(8,128)(2,1)} %copy-done.15) | copy-start | bytes 69124
  62.5 4.0 copy-start.47
  62.5 10.9 %copy-start.3 = (bf16[768,1536]{0,1:T(8,128)(2,1)}, bf16[768,1536]{0,1:T(8,128)(2,1)S(1)}, u32[]{:S(2)}) copy-start(bf16[768,1536]{0,1:T(8,128)(2,1)S(1)} %get-tuple-element.225) | copy-start | bytes 7077892
  62.6 6.0 %collective-permute-start.5 = (bf16[15,768]{1,0:T(8,128)(2,1)S(1)}, bf16[15,768]{1,0:T(8,128)(2,1)S(1)}, u32[]{:S(2)}, u32[]{:S(2)}) collective-permute-start(bf16[15,768]{1,0:T(8,128)(2,1)S(1)} %get-tuple-element.477), channel_id=1, source_target_pairs={{0,1},{1,2},{2,3},{3,4},{4,5},{5,6},{6,7},{7,8},{8,9},{9,10},{10,1... | collective-permute-start | bytes 69128 | tf_op jit(solution)/shard_map/ppermute | solution.py:16
  66.5 6.9 %collective-permute-start.6 = (bf16[15,768]{1,0:T(8,128)(2,1)S(1)}, bf16[15,768]{1,0:T(8,128)(2,1)S(1)}, u32[]{:S(2)}, u32[]{:S(2)}) collective-permute-start(bf16[15,768]{1,0:T(8,128)(2,1)S(1)} %get-tuple-element.478), channel_id=1, source_target_pairs={{1,0},{2,1},{3,2},{4,3},{5,4},{6,5},{7,6},{8,7},{9,8},{10,9},{11,1... | collective-permute-start | bytes 69128 | tf_op jit(solution)/shard_map/ppermute | solution.py:17
  74.6 57.5 %copy-start = (bf16[1536,1536]{0,1:T(8,128)(2,1)}, bf16[1536,1536]{0,1:T(8,128)(2,1)S(1)}, u32[]{:S(2)}) copy-start(bf16[1536,1536]{0,1:T(8,128)(2,1)S(1)} %get-tuple-element.217) | copy-start | bytes 14155780
  74.6 57.5 %copy-start.27 = (bf16[1536]{0:T(1024)(128)(2,1)}, bf16[1536]{0:T(1024)(128)(2,1)S(1)}, u32[]{:S(2)}) copy-start(bf16[1536]{0:T(1024)(128)(2,1)S(1)} %get-tuple-element.221) | copy-start | bytes 9220
  74.6 57.5 %copy-start.11 = (bf16[128,1536]{1,0:T(8,128)(2,1)}, bf16[128,1536]{1,0:T(8,128)(2,1)S(1)}, u32[]{:S(2)}) copy-start(bf16[128,1536]{1,0:T(8,128)(2,1)S(1)} %get-tuple-element.212) | copy-start | bytes 1179652
  74.6 57.5 %collective-permute-start.7 = (bf16[128,1536]{1,0:T(8,128)(2,1)S(1)}, bf16[128,1536]{1,0:T(8,128)(2,1)S(1)}, u32[]{:S(2)}, u32[]{:S(2)}) collective-permute-start(bf16[128,1536]{1,0:T(8,128)(2,1)S(1)} %get-tuple-element.212), channel_id=1, source_target_pairs={{32,0},{33,1},{34,2},{35,3},{36,4},{37,5},{38,6},{39,7},{40,8},{41... | collective-permute-start | bytes 1179656 | tf_op jit(solution)/shard_map/ppermute | solution.py:25
  134.2 3.9 copy-start.24
  138.0 3.5 copy-start.49
  158.0 9.2 %copy-start.21 = (f32[128,1]{0,1:T(1,128)S(1)}, f32[128,1]{0,1:T(1,128)}, u32[]{:S(2)}) copy-start(f32[128,1]{0,1:T(1,128)} %copy-done.20) | copy-start | bytes 1540
  158.1 248.2 %reduce-scatter.8.cloned.1.call-start = ((), (), s32[]{:S(2)}) async-start(), calls=%async_computation.4 | async-start | bytes 6488064 | tf_op jit(solution)/shard_map/reduce_scatter | solution.py:215
  158.2 4.9 %collective-permute-start.8 = (bf16[15,768]{1,0:T(8,128)(2,1)S(1)}, bf16[15,768]{1,0:T(8,128)(2,1)S(1)}, u32[]{:S(2)}, u32[]{:S(2)}) collective-permute-start(bf16[15,768]{1,0:T(8,128)(2,1)S(1)} %get-tuple-element.475), channel_id=1, source_target_pairs={{0,1},{1,2},{2,3},{3,4},{4,5},{5,6},{6,7},{7,8},{8,9},{9,10},{10,1... | collective-permute-start | bytes 69128 | tf_op jit(solution)/shard_map/ppermute | solution.py:16
  161.1 6.1 %collective-permute-start.9 = (bf16[15,768]{1,0:T(8,128)(2,1)S(1)}, bf16[15,768]{1,0:T(8,128)(2,1)S(1)}, u32[]{:S(2)}, u32[]{:S(2)}) collective-permute-start(bf16[15,768]{1,0:T(8,128)(2,1)S(1)} %get-tuple-element.476), channel_id=1, source_target_pairs={{1,0},{2,1},{3,2},{4,3},{5,4},{6,5},{7,6},{8,7},{9,8},{10,9},{11,1... | collective-permute-start | bytes 69128 | tf_op jit(solution)/shard_map/ppermute | solution.py:17
  209.8 0.7 copy-start.52
  209.8 1.3 copy-start.51
  209.8 1.9 copy-start.10
  209.8 3.6 copy-start.48
  209.8 3.8 copy-start.28
  209.8 125.5 %copy-start.12 = (bf16[128,1536]{1,0:T(8,128)(2,1)S(1)}, bf16[128,1536]{1,0:T(8,128)(2,1)}, u32[]{:S(2)}) copy-start(bf16[128,1536]{1,0:T(8,128)(2,1)} %copy-done.11) | copy-start | bytes 1179652
  209.8 222.0 %reduce-scatter.14.cloned.1.call-start = ((), (), s32[]{:S(2)}) async-start(), calls=%async_computation.7 | async-start | bytes 122880 | tf_op jit(solution)/shard_map/reduce_scatter | solution.py:234
  337.1 119.9 %reduce-scatter.10.cloned.1.call-start = ((), (), s32[]{:S(2)}) async-start(), calls=%async_computation.5 | async-start | bytes 245760 | tf_op jit(solution)/shard_map/reduce_scatter | solution.py:222
Sparse Core Ops, SparseCore 0:
  158.2 120.3 reduce-scatter.11
  281.4 124.9 reduce-scatter.7
  409.0 22.8 reduce-scatter.13
  434.2 22.8 reduce-scatter.9
where the time goes:
time: 469 us; the launch traced here: 465 us
  waiting for transfers between devices  192 us (41%)
  blocking collectives  118 us (25%)
  local copies, waits for them, and re-layouts  52.6 us (11%)
  other arithmetic  41.1 us (9%)
  starting transfers between devices  24.2 us (5%)
  matrix products  21 us (4%)
  between operations  15 us (3%)
    unnamed x2, blocking collectives  118 us
    reduce_scatter x1, waiting for transfers between devices, per_device(): lax.psum_scatter(term_one, 'tm', scatter_dimension=2, tiled=True)  66.3 us
    ppermute x2, waiting for transfers between devices, passed_along(): return lax.ppermute(shard, axis, pairs)  63.5 us
    reduce_scatter x1, waiting for transfers between devices, per_device(): lax.psum_scatter(shares[4].astype(jnp.bfloat16), 'dp', scatter_dimension=...  25.5 us
    reduce_scatter x1, waiting for transfers between devices, per_device(): lax.psum_scatter(shares[0].astype(jnp.bfloat16), 'dp', scatter_dimension=...  23.8 us
    reshape x2, local copies, waits for them, and re-layouts, per_device(): grad_one.astype(jnp.bfloat16)  14.2 us
    ppermute x4, starting transfers between devices, extended(): before = lax.ppermute(last, axis, up)  13.4 us
    ppermute x4, waiting for transfers between devices, extended(): after = lax.ppermute(first, axis, down)  12.7 us
  transfers between devices with their start and end apart: 14, of which 9 were waited for; matrix products, arithmetic and copies ran while one was open for 12% of the time, Pallas kernels for 0%

commit v1 on v0

v1 whole, which is shorter than its diff:
```python
import functools

import jax
import jax.numpy as jnp
from jax import lax
from jax.experimental import pallas as pl
from jax.experimental.pallas import tpu as pltpu
from jax.sharding import PartitionSpec as P

EPS = 1e-05
F32 = jnp.float32
BF16 = jnp.bfloat16
MESH = pl.DeviceIdType.MESH
NT = (((1,), (1,)), ((), ()))
HALO = 16
TAPS = 31
LANE = 128
ROWS = 32


def dot(a, b):
    return jnp.dot(a, b, preferred_element_type=F32)


def dot_t(a, b):
    return lax.dot_general(a, b, NT, preferred_element_type=F32)


def kernel(
    n_y,
    n_z,
    n_tm,
    len_ref,
    inp,
    gout,
    w1,
    w2,
    kern,
    gain1,
    gain2,
    out_ref,
    grad_ref,
    o_one,
    o_two,
    o_small,
    cur,
    e,
    xhat,
    rstd1,
    normed,
    p_buf,
    sig_buf,
    gpad,
    dpad,
    conv,
    zhat,
    rstd2,
    zn_buf,
    act,
    d_act,
    d_norm,
    edge_g,
    edge_d,
    halo_g,
    halo_d,
    dout4,
    dpre4,
    dout_r,
    dpre_r,
    n_t,
    a_t,
    gk,
    gg1,
    ebuf,
    tbuf,
    pa,
    pb,
    ya,
    yb,
    qa,
    qb,
    za,
    zb,
    fs,
    fr,
    sem_h,
    sem_out,
    sem_grad,
    sem_x,
    sem_y,
    sem_z,
    sem_f,
):
    frames, model = inp.shape
    width = w2.shape[0]
    dy = lax.axis_index("dp")
    seg = lax.axis_index("segment")
    t = lax.axis_index("tm")
    c = t % 2
    xl = (t // 2) % 2
    z = t // 4
    j = t % 4
    base = z * 4
    group = [base + xl * 2 + (1 - c), base + (1 - xl) * 2 + c, base + (1 - xl) * 2 + (1 - c)]
    right = (t + 1) % n_tm
    left = (t + n_tm - 1) % n_tm
    first_seg = seg == 0
    last_seg = seg == 1

    def remote(src, dst, sems, index, axis, peer):
        return pltpu.make_async_remote_copy(
            src_ref=src,
            dst_ref=dst,
            send_sem=sems.at[0, index],
            recv_sem=sems.at[1, index],
            device_id={axis: peer},
            device_id_type=MESH,
        )

    barrier = pltpu.get_barrier_semaphore()
    greet = [("tm", left), ("tm", right), ("segment", 1 - seg)]
    greet += [("tm", g) for g in group]
    greet += [("dp", (dy + d) % n_y) for d in range(1, n_y)]
    greet += [("tm", ((z + d) % n_z) * 4 + j) for d in range(1, n_z)]
    for axis, peer in greet:
        pl.semaphore_signal(barrier, inc=1, device_id={axis: peer}, device_id_type=MESH)

    length = len_ref[0]

    def mask_of(start, rows):
        ids = t * frames + start + lax.broadcasted_iota(jnp.int32, (rows, 1), 0)
        return (ids < length).astype(F32)

    def over_rows(work):
        def step(i, carry):
            start = pl.multiple_of(i * ROWS, ROWS)
            work(start, pl.ds(start, ROWS))
            return carry

        lax.fori_loop(0, frames // ROWS, step, 0)

    def out_copies():
        return [
            remote(
                out_ref.at[pl.ds(64 * i, 64)], cur.at[pl.ds(64 * i, 64)], sem_out, i, "segment", 1 - seg
            )
            for i in range(2)
        ]

    def grad_copies():
        return [
            remote(
                grad_ref.at[pl.ds(64 * i, 64)], e.at[pl.ds(64 * i, 64)], sem_grad, i, "segment", 1 - seg
            )
            for i in range(2)
        ]

    def halo_copies(edge, halo, offset):
        return [
            remote(edge.at[0], halo.at[1], sem_h, offset, "tm", left),
            remote(edge.at[1], halo.at[0], sem_h, offset + 1, "tm", right),
        ]

    def peer_j(d):
        return group[d] % 4

    def dout_copies():
        return [
            remote(dout4.at[peer_j(d)], dout_r.at[d], sem_x, d, "tm", group[d]) for d in range(3)
        ]

    def dpre_copies():
        return [
            remote(dpre4.at[peer_j(d)], dpre_r.at[d], sem_x, 3 + d, "tm", group[d]) for d in range(3)
        ]

    def turned_copies():
        return [
            remote(n_t.at[0], n_t.at[d + 1], sem_x, 6 + d, "tm", group[d]) for d in range(3)
        ] + [remote(a_t.at[0], a_t.at[d + 1], sem_x, 9 + d, "tm", group[d]) for d in range(3)]

    def start_all(copies):
        for copy in copies:
            copy.start()

    def upper():
        def mask_rows(start, rows):
            d_out = (e[rows, :].astype(F32) * mask_of(start, ROWS)).astype(BF16)
            for i in range(4):
                dout4[i, rows, :] = d_out[:, 384 * i : 384 * (i + 1)]

        over_rows(mask_rows)
        d_out = jnp.concatenate([dout4[i] for i in range(4)], axis=1)
        for n in range(width // 256):
            d_act[:, 256 * n : 256 * (n + 1)] = dot_t(d_out, w2[256 * n : 256 * (n + 1), :])

    def taps_over(src, block, flip):
        cols = pl.ds(pl.multiple_of(block * LANE, LANE), LANE)
        whole = src[:, cols]
        total = jnp.zeros((frames, LANE), F32)
        for r in range(8):
            moved = whole if r == 0 else pltpu.roll(whole, whole.shape[0] - r, 0)
            for k in range(TAPS):
                if (k + 1) % 8 == r:
                    at = k + 1 - r
                    tap = TAPS - 1 - k if flip else k
                    total = total + kern[tap : tap + 1, cols] * moved[at : at + frames]
        return cols, total

    def turn():
        for i in range(model // LANE):
            cols = slice(LANE * i, LANE * (i + 1))
            n_t[0, cols, :] = normed[:, cols].astype(F32).T.astype(BF16)
        for i in range(width // LANE):
            cols = slice(LANE * i, LANE * (i + 1))
            a_t[0, cols, :] = act[:, cols].astype(F32).T.astype(BF16)

    @pl.when(last_seg)
    def _():
        e[...] = gout[...]
        upper()

    pl.semaphore_wait(barrier, len(greet))

    @pl.when(last_seg)
    def _():
        start_all(dout_copies())
        for copy in out_copies():
            copy.wait_recv()

    @pl.when(first_seg)
    def _():
        cur[...] = inp[...]

    def norm_rows(start, rows):
        x = cur[rows, :].astype(F32)
        centred = x - jnp.mean(x, axis=-1, keepdims=True)
        rstd = lax.rsqrt(jnp.mean(centred * centred, axis=-1, keepdims=True) + EPS)
        hat = centred * rstd
        xhat[rows, :] = hat
        rstd1[rows, :] = jnp.broadcast_to(rstd, (ROWS, LANE))
        normed[rows, :] = (hat * gain1[...]).astype(BF16)

    over_rows(norm_rows)
    maskf = mask_of(0, frames)
    for n in range(width // 256):
        cols = slice(256 * n, 256 * (n + 1))
        q_cols = slice(width + 256 * n, width + 256 * (n + 1))
        p = dot(normed[...], w1[:, cols])
        sig = jax.nn.sigmoid(dot(normed[...], w1[:, q_cols]))
        p_buf[:, cols] = p
        sig_buf[:, cols] = sig
        gated = (p * sig * maskf).astype(BF16)
        gpad[HALO : HALO + frames, cols] = gated.astype(F32)
        edge_g[0, :, cols] = gated[:HALO]
        edge_g[1, :, cols] = gated[frames - HALO :]
    copies = halo_copies(edge_g, halo_g, 0)
    start_all(copies)
    for copy in copies:
        copy.wait()
    has_left = (t > 0).astype(F32)
    has_right = (t < n_tm - 1).astype(F32)
    gpad[0:HALO, :] = halo_g[0].astype(F32) * has_left
    gpad[HALO + frames :, :] = halo_g[1].astype(F32) * has_right

    def conv_block(block, carry):
        cols, total = taps_over(gpad, block, False)
        conv[:, cols] = total
        return carry

    lax.fori_loop(0, width // LANE, conv_block, 0)

    def act_rows(start, rows):
        x = conv[rows, :]
        centred = x - jnp.mean(x, axis=-1, keepdims=True)
        rstd = lax.rsqrt(jnp.mean(centred * centred, axis=-1, keepdims=True) + EPS)
        hat = centred * rstd
        zn = hat * gain2[...]
        zhat[rows, :] = hat
        zn_buf[rows, :] = zn
        rstd2[rows, :] = jnp.broadcast_to(rstd, (ROWS, LANE))
        act[rows, :] = (zn * jax.nn.sigmoid(zn)).astype(BF16)

    over_rows(act_rows)
    for n in range(model // 512):
        cols = slice(512 * n, 512 * (n + 1))
        out = dot(act[...], w2[:, cols])
        out_ref[:, cols] = (cur[:, cols].astype(F32) + maskf * out).astype(BF16)

    @pl.when(first_seg)
    def _():
        copies = out_copies()
        start_all(copies)
        turn()
        for copy in copies:
            copy.wait_send()
        start_all(turned_copies())
        for copy in grad_copies():
            copy.wait_recv()
        upper()

    gg1[...] = jnp.zeros_like(gg1)
    gk[...] = jnp.zeros_like(gk)

    def conv_grad_rows(start, rows):
        zn = zn_buf[rows, :]
        hat = zhat[rows, :]
        sg = jax.nn.sigmoid(zn)
        d_zn = d_act[rows, :] * (sg + zn * sg * (1.0 - sg))
        gk[TAPS : TAPS + 1, :] += jnp.sum(d_zn * hat, axis=0, keepdims=True)
        d_hat = d_zn * gain2[...]
        m_one = jnp.mean(d_hat, axis=-1, keepdims=True)
        m_two = jnp.mean(d_hat * hat, axis=-1, keepdims=True)
        d_conv = rstd2[rows, 0:1] * (d_hat - m_one - hat * m_two)
        dpad[pl.ds(HALO + start, ROWS), :] = d_conv

    over_rows(conv_grad_rows)
    edge_d[0] = dpad[HALO : 2 * HALO, :].astype(BF16)
    edge_d[1] = dpad[frames : HALO + frames, :].astype(BF16)
    copies = halo_copies(edge_d, halo_d, 2)
    start_all(copies)

    @pl.when(first_seg)
    def _():
        start_all(dout_copies())

    def tap_grads(block, carry):
        cols = pl.ds(pl.multiple_of(block * LANE, LANE), LANE)
        whole = gpad[:, cols]
        d_conv = dpad[HALO : HALO + frames, cols]
        for r in range(8):
            moved = whole if r == 0 else pltpu.roll(whole, whole.shape[0] - r, 0)
            for k in range(TAPS):
                if (k + 1) % 8 == r:
                    at = k + 1 - r
                    gk[k : k + 1, cols] = jnp.sum(
                        moved[at : at + frames] * d_conv, axis=0, keepdims=True
                    )
        return carry

    lax.fori_loop(0, width // LANE, tap_grads, 0)
    for copy in copies:
        copy.wait()
    dpad[0:HALO, :] = halo_d[0].astype(F32) * has_left
    dpad[HALO + frames :, :] = halo_d[1].astype(F32) * has_right

    for half in range(2):

        def pre_block(block, carry):
            cols, total = taps_over(dpad, half * 3 + block, True)
            d_gated = total * maskf
            sig = sig_buf[:, cols]
            d_p = d_gated * sig
            d_q = d_p * p_buf[:, cols] * (1.0 - sig)
            part = pl.ds(pl.multiple_of(block * LANE, LANE), LANE)
            dpre4[half, :, part] = d_p.astype(BF16)
            dpre4[2 + half, :, part] = d_q.astype(BF16)
            return carry

        lax.fori_loop(0, 3, pre_block, 0)

    @pl.when(first_seg)
    def _():
        start_all(dpre_copies())

    d_pre = jnp.concatenate([dpre4[i] for i in range(4)], axis=1)
    for n in range(model // 512):
        rows = slice(512 * n, 512 * (n + 1))
        d_norm[:, rows] = dot_t(d_pre, w1[rows, :])

    def grad_rows(start, rows):
        d_normed = d_norm[rows, :]
        hat = xhat[rows, :]
        gg1[0:1, :] += jnp.sum(d_normed * hat, axis=0, keepdims=True)
        d_hat = d_normed * gain1[...]
        m_one = jnp.mean(d_hat, axis=-1, keepdims=True)
        m_two = jnp.mean(d_hat * hat, axis=-1, keepdims=True)
        d_h = rstd1[rows, 0:1] * (d_hat - m_one - hat * m_two)
        grad_ref[rows, :] = (e[rows, :].astype(F32) + d_h).astype(BF16)

    over_rows(grad_rows)

    @pl.when(last_seg)
    def _():
        copies = grad_copies()
        start_all(copies)
        turn()
        for copy in copies:
            copy.wait_send()
        start_all(dpre_copies())
        start_all(turned_copies())

    for i in range(width // LANE):
        cols = slice(LANE * i, LANE * (i + 1))
        ebuf[cols, :] = gk[:, cols].T
    for i in range(model // LANE):
        cols = slice(LANE * i, LANE * (i + 1))
        tbuf[cols, :] = jnp.broadcast_to(gg1[0:1, cols], (LANE, LANE)).T

    for copy in dpre_copies() + turned_copies() + dout_copies():
        copy.wait()
    own_pre = dpre4[j]
    rhs_one = jnp.concatenate([own_pre] + [dpre_r[d] for d in range(3)], axis=0)

    def y_copy(buf, got, d, offset):
        peer = (dy + d) % n_y
        return remote(buf.at[peer], got.at[d - 1], sem_y, offset + d - 1, "dp", peer)

    def z_copy(buf, got, d, offset):
        peer = (z + d) % n_z
        return remote(buf.at[peer], got.at[d - 1], sem_z, offset + d - 1, "tm", peer * 4 + j)

    y_order = list(range(1, n_y)) + [0]
    rows_one = model // n_y
    rows_two = width // n_y
    for d in y_order:
        peer = (dy + d) % n_y
        start = pl.multiple_of(peer * rows_one, rows_one)
        lhs = jnp.concatenate([n_t[i, pl.ds(start, rows_one), :] for i in range(4)], axis=1)
        part = dot(lhs, rhs_one)
        for i in range(n_z):
            pa[peer, i] = part[48 * i : 48 * (i + 1)].astype(BF16)
        if d:
            y_copy(pa, ya, d, 0).start()

    rhs_two = jnp.concatenate([dout4[j]] + [dout_r[d] for d in range(3)], axis=0)
    lane = lax.broadcasted_iota(jnp.int32, (24, LANE), 1)
    for d in y_order:
        peer = (dy + d) % n_y
        start = pl.multiple_of(peer * rows_two, rows_two)
        lhs = jnp.concatenate([a_t[i, pl.ds(start, rows_two), :] for i in range(4)], axis=1)
        part = dot(lhs, rhs_two)
        for i in range(n_z):
            at = pl.multiple_of(peer * rows_two + 24 * i, 8)
            at_t = pl.multiple_of(peer * rows_one + 48 * i, 8)
            extra = ebuf[pl.ds(at, 24), :]
            extra = jnp.where(lane == 32, tbuf[pl.ds(at_t, 24), :], extra)
            extra = jnp.where(lane == 33, tbuf[pl.ds(at_t + 24, 24), :], extra)
            mine = part[24 * i : 24 * (i + 1)]
            low = jnp.concatenate([mine[:, 256:], extra], axis=1)
            pb[peer, i] = jnp.concatenate([mine[:, :256], low], axis=0).astype(BF16)
        if d:
            y_copy(pb, yb, d, n_y - 1).start()

    for buf, got, q_buf, z_got, off_y, off_z in (
        (pa, ya, qa, za, 0, 0),
        (pb, yb, qb, zb, n_y - 1, n_z - 1),
    ):
        for d in range(1, n_y):
            y_copy(buf, got, d, off_y).wait()
        for i in range(n_z):
            total = buf[dy, i].astype(F32)
            for d in range(n_y - 1):
                total = total + got[d, i].astype(F32)
            q_buf[i] = total.astype(BF16)
        for d in range(1, n_z):
            z_copy(q_buf, z_got, d, off_z).start()

    fs[...] = jnp.zeros_like(fs)
    for d in range(1, n_z):
        z_copy(qa, za, d, 0).wait()
    total = qa[z].astype(F32)
    for d in range(n_z - 1):
        total = total + za[d].astype(F32)
    for i in range(4):
        fs[i, 0:12, :] = total[12 * i : 12 * (i + 1)]
    for d in range(1, n_z):
        z_copy(qb, zb, d, n_z - 1).wait()
    total = qb[z].astype(F32)
    for d in range(n_z - 1):
        total = total + zb[d].astype(F32)
    two = jnp.concatenate([total[:24], total[24:, :LANE]], axis=1)
    extra = total[24:, LANE:]
    for i in range(4):
        fs[i, 16:22, :] = two[6 * i : 6 * (i + 1)]
        for m in range(3):
            fs[i, 24:32, LANE * m : LANE * (m + 1)] = extra[8 * m : 8 * (m + 1)]
    copies = [remote(fs.at[peer_j(d)], fr.at[j], sem_f, d, "tm", group[d]) for d in range(3)]
    start_all(copies)
    fr[j] = fs[j]
    for copy in copies:
        copy.wait()
    small = jnp.zeros((8, 3 * LANE), F32)
    for i in range(4):
        cols = slice(384 * i, 384 * (i + 1))
        o_one[:, cols] = fr[i, 0:12, :]
        o_two[:, cols] = fr[i, 16:22, :]
        small = small + fr[i, 24:32, :]
    for m in range(3):
        o_small[8 * m : 8 * (m + 1), :] = small[:, LANE * m : LANE * (m + 1)]


def per_device(inputs, lengths, w_first, kernel_w, gain_first, gain_second, w_second, grad_output):
    n_y = lax.axis_size("dp")
    n_tm = lax.axis_size("tm")
    n_z = n_tm // 4
    frames, model = inputs.shape[1:]
    width = w_second.shape[1]
    groups = n_y * n_tm
    vmem = pl.BlockSpec(memory_space=pltpu.VMEM)

    def buf(shape, dtype):
        return pltpu.VMEM(shape, dtype)

    wide = (frames, model)
    thin = (frames, width)
    padded = (frames + 2 * HALO, width)
    third = (4, frames, 384)
    scratch = [
        buf(wide, BF16),
        buf(wide, BF16),
        buf(wide, F32),
        buf((frames, LANE), F32),
        buf(wide, BF16),
        buf(thin, F32),
        buf(thin, F32),
        buf(padded, F32),
        buf(padded, F32),
        buf(thin, F32),
        buf(thin, F32),
        buf((frames, LANE), F32),
        buf(thin, F32),
        buf(thin, BF16),
        buf(thin, F32),
        buf(wide, F32),
        buf((2, HALO, width), BF16),
        buf((2, HALO, width), BF16),
        buf((2, HALO, width), BF16),
        buf((2, HALO, width), BF16),
        buf(third, BF16),
        buf(third, BF16),
        buf((3, frames, 384), BF16),
        buf((3, frames, 384), BF16),
        buf((4, model, LANE), BF16),
        buf((4, width, LANE), BF16),
        buf((LANE, width), F32),
        buf((8, model), F32),
        buf((width, LANE), F32),
        buf((model, LANE), F32),
        buf((n_y, n_z, 48, 384), BF16),
        buf((n_y, n_z, 48, 256), BF16),
        buf((n_y - 1, n_z, 48, 384), BF16),
        buf((n_y - 1, n_z, 48, 256), BF16),
        buf((n_z, 48, 384), BF16),
        buf((n_z, 48, 256), BF16),
        buf((n_z - 1, 48, 384), BF16),
        buf((n_z - 1, 48, 256), BF16),
        buf((4, 32, 384), F32),
        buf((4, 32, 384), F32),
        pltpu.SemaphoreType.DMA((2, 4)),
        pltpu.SemaphoreType.DMA((2, 2)),
        pltpu.SemaphoreType.DMA((2, 2)),
        pltpu.SemaphoreType.DMA((2, 12)),
        pltpu.SemaphoreType.DMA((2, 2 * (n_y - 1))),
        pltpu.SemaphoreType.DMA((2, 2 * (n_z - 1))),
        pltpu.SemaphoreType.DMA((2, 3)),
    ]
    out, grad, one, two, small = pl.pallas_call(
        functools.partial(kernel, n_y, n_z, n_tm),
        out_shape=(
            jax.ShapeDtypeStruct(wide, BF16),
            jax.ShapeDtypeStruct(wide, BF16),
            jax.ShapeDtypeStruct((model // groups, model), F32),
            jax.ShapeDtypeStruct((width // groups, model), F32),
            jax.ShapeDtypeStruct((24, LANE), F32),
        ),
        in_specs=[pl.BlockSpec(memory_space=pltpu.SMEM)] + [vmem] * 7,
        out_specs=(vmem,) * 5,
        scratch_shapes=scratch,
        compiler_params=pltpu.CompilerParams(
            collective_id=0, has_side_effects=True, vmem_limit_bytes=60 * 1024 * 1024
        ),
        cost_estimate=pl.CostEstimate(
            flops=2 * 3 * frames * model * 3 * width, bytes_accessed=12_000_000, transcendentals=0
        ),
    )(
        lengths,
        inputs[0],
        grad_output[0],
        w_first[0],
        w_second[0],
        kernel_w[0],
        gain_first,
        gain_second,
    )
    j = lax.axis_index("tm") % 4
    mine = lax.dynamic_slice(small, (6 * j, 0), (6, LANE))
    g_one = lax.dynamic_slice(small[:, 32:34].T.reshape(48), (12 * j,), (12,))
    return (
        out[None, None],
        grad[None, None],
        one[None],
        mine[:, :TAPS].T[None],
        g_one[None],
        mine[:, TAPS][None],
        two[None],
    )


def solution(mesh):
    in_specs = (
        P("dp", "tm", None),
        P("dp"),
        P("segment", None, None),
        P("segment", None, None),
        P("segment", None),
        P("segment", None),
        P("segment", None, None),
        P("dp", "tm", None),
    )
    out_specs = (
        P("segment", "dp", "tm", None),
        P("segment", "dp", "tm", None),
        P("segment", ("dp", "tm"), None),
        P("segment", None, ("dp", "tm")),
        P("segment", ("dp", "tm")),
        P("segment", ("dp", "tm")),
        P("segment", ("dp", "tm"), None),
    )
    return jax.shard_map(
        per_device, mesh=mesh, in_specs=in_specs, out_specs=out_specs, check_vma=False
    )
```

time: 469 us -> 132 us (0.28)
  the two profiles are of different devices: /device:TPU:1 before, /device:TPU:7 now
where the time goes in v1:
time: 132 us
  Pallas kernels  119 us (90%)
  local copies, waits for them, and re-layouts  11.6 us (9%)
  between operations  1.32 us (1%)
    pallas_call x1, Pallas kernels, per_device(): pl.pallas_call(functools.partial(kernel, n_y, n_z, n_tm), out_shape=(jax....  119 us
    unnamed x6, local copies, waits for them, and re-layouts  8.71 us

profile of v1, /device:TPU:7, one launch (start us, length us, event | category | flops | bytes accessed | tf_op | source)
XLA Modules:
  0.0 131.9 jit_solution(13224791171062129083)
XLA Ops:
  0.7 1.5 %copy.25 = f32[1,31,768]{2,1,0:T(8,128)} copy(f32[1,31,768]{2,0,1:T(1,128)} %param.11) | data formatting | bytes 190464
  2.8 118.9 %shard_map.135 = (bf16[128,1536]{1,0:T(8,128)(2,1)}, bf16[128,1536]{1,0:T(8,128)(2,1)}, f32[12,1536]{1,0:T(8,128)}, f32[6,1536]{1,0:T(8,128)}, f32[24,128]{1,0:T(8,128)}) custom-call(s32[1]{0:T(128)S(6)} %copy.28.len_ref, bf16[128,1536]{1,0:T(8,128)(2,1)} %bitcast.28, bf16[128,1536]{1,0:T(8,128)(2,1)} %bitcast.29, bf16[1536,1536]{1,0:T(8,128)(2,1)} %bitcast.26, ...), custom_call_target="tpu_custom_call" | custom-call | flops 2717908992 | bytes 12000000 | tf_op jit(solution)/shard_map/pallas_call | solution.py:558
  121.8 0.8 slice_bitcast_fusion
  122.5 0.1 copy.19
  122.6 0.1 reshape.17
  122.7 0.6 dynamic-slice_bitcast_fusion
  123.3 0.7 constant_dynamic-slice_fusion
  124.0 0.6 copy.21
  124.6 0.7 slice_reduce_fusion
  125.3 1.6 %copy.20 = f32[1,12,1536]{2,0,1:T(1,128)} copy(f32[1,12,1536]{2,1,0:T(8,128)} %bitcast.23) | data formatting | bytes 147456
  126.9 1.5 %copy.22 = f32[1,6,1536]{2,0,1:T(1,128)} copy(f32[1,6,1536]{2,1,0:T(8,128)} %bitcast.24) | data formatting | bytes 73728
  128.3 1.8 %copy.29 = bf16[1,1,128,1536]{3,2,1,0:T(8,128)(2,1)} copy(bf16[1,1,128,1536]{3,2,1,0:T(8,128)(2,1)} %bitcast.21) | data formatting | bytes 786432
  130.1 1.8 %copy.30 = bf16[1,1,128,1536]{3,2,1,0:T(8,128)(2,1)} copy(bf16[1,1,128,1536]{3,2,1,0:T(8,128)(2,1)} %bitcast.20) | data formatting | bytes 786432
  (1 shorter events, 0.0 us)

commit v2 on v1

--- a/solution.py
+++ b/solution.py
@@ -33,16 +33,22 @@
     len_ref,
     inp,
     gout,
-    w1,
-    w2,
+    w1_hbm,
+    w2_hbm,
     kern,
     gain1,
     gain2,
+    out_hbm,
+    grad_hbm,
+    o_one,
+    o_two,
+    o_kern,
+    o_gain1,
+    o_gain2,
+    w1,
+    w2,
     out_ref,
     grad_ref,
-    o_one,
-    o_two,
-    o_small,
     cur,
     e,
     xhat,
@@ -75,6 +81,8 @@
     tbuf,
     pa,
     pb,
+    ya_in,
+    yb_in,
     ya,
     yb,
     qa,
@@ -83,6 +91,7 @@
     zb,
     fs,
     fr,
+    sem_w,
     sem_h,
     sem_out,
     sem_grad,
@@ -117,6 +126,10 @@
             device_id_type=MESH,
         )
 
+    load_w1 = pltpu.make_async_copy(w1_hbm, w1, sem_w.at[0])
+    load_w2 = pltpu.make_async_copy(w2_hbm, w2, sem_w.at[1])
+    store_out = pltpu.make_async_copy(out_ref, out_hbm, sem_w.at[2])
+    store_grad = pltpu.make_async_copy(grad_ref, grad_hbm, sem_w.at[3])
     barrier = pltpu.get_barrier_semaphore()
     greet = [("tm", left), ("tm", right), ("segment", 1 - seg)]
     greet += [("tm", g) for g in group]
@@ -125,6 +138,16 @@
     for axis, peer in greet:
         pl.semaphore_signal(barrier, inc=1, device_id={axis: peer}, device_id_type=MESH)
 
+    @pl.when(first_seg)
+    def _():
+        load_w1.start()
+        load_w2.start()
+
+    @pl.when(last_seg)
+    def _():
+        load_w2.start()
+        load_w1.start()
+
     length = len_ref[0]
 
     def mask_of(start, rows):
@@ -174,10 +197,23 @@
             remote(dpre4.at[peer_j(d)], dpre_r.at[d], sem_x, 3 + d, "tm", group[d]) for d in range(3)
         ]
 
-    def turned_copies():
-        return [
-            remote(n_t.at[0], n_t.at[d + 1], sem_x, 6 + d, "tm", group[d]) for d in range(3)
-        ] + [remote(a_t.at[0], a_t.at[d + 1], sem_x, 9 + d, "tm", group[d]) for d in range(3)]
+    mid = model // 2
+
+    def turned_copies(part, forward=False):
+        buf = a_t if part == 2 else n_t
+        rows = pl.ds(mid * part if part < 2 else 0, mid)
+
+        def one(src, dst, d):
+            return remote(
+                buf.at[src, rows], buf.at[dst, rows], sem_x, 6 + 3 * part + d, "tm", group[d % 2]
+            )
+
+        return [one(2, 3, 2)] if forward else [one(0, 1, 0), one(0, 2, 1)]
+
+    def forward_turned():
+        for part in range(3):
+            turned_copies(part)[1].wait_recv()
+            turned_copies(part, True)[0].start()
 
     def start_all(copies):
         for copy in copies:
@@ -204,13 +240,15 @@
                 if (k + 1) % 8 == r:
                     at = k + 1 - r
                     tap = TAPS - 1 - k if flip else k
-                    total = total + kern[tap : tap + 1, cols] * moved[at : at + frames]
+                    total = total + kern[tap, :, cols] * moved[at : at + frames]
         return cols, total
 
-    def turn():
+    def turn_normed():
         for i in range(model // LANE):
             cols = slice(LANE * i, LANE * (i + 1))
             n_t[0, cols, :] = normed[:, cols].astype(F32).T.astype(BF16)
+
+    def turn_act():
         for i in range(width // LANE):
             cols = slice(LANE * i, LANE * (i + 1))
             a_t[0, cols, :] = act[:, cols].astype(F32).T.astype(BF16)
@@ -218,6 +256,7 @@
     @pl.when(last_seg)
     def _():
         e[...] = gout[...]
+        load_w2.wait()
         upper()
 
     pl.semaphore_wait(barrier, len(greet))
@@ -242,6 +281,7 @@
         normed[rows, :] = (hat * gain1[...]).astype(BF16)
 
     over_rows(norm_rows)
+    load_w1.wait()
     maskf = mask_of(0, frames)
     for n in range(width // 256):
         cols = slice(256 * n, 256 * (n + 1))
@@ -256,6 +296,8 @@
         edge_g[1, :, cols] = gated[frames - HALO :]
     copies = halo_copies(edge_g, halo_g, 0)
     start_all(copies)
+    turn_normed()
+    start_all(turned_copies(0))
     for copy in copies:
         copy.wait()
     has_left = (t > 0).astype(F32)
@@ -282,6 +324,11 @@
         act[rows, :] = (zn * jax.nn.sigmoid(zn)).astype(BF16)
 
     over_rows(act_rows)
+
+    @pl.when(first_seg)
+    def _():
+        load_w2.wait()
+
     for n in range(model // 512):
         cols = slice(512 * n, 512 * (n + 1))
         out = dot(act[...], w2[:, cols])
@@ -291,10 +338,13 @@
     def _():
         copies = out_copies()
         start_all(copies)
-        turn()
+        store_out.start()
+        turn_act()
         for copy in copies:
             copy.wait_send()
-        start_all(turned_copies())
+        start_all(turned_copies(1))
+        start_all(turned_copies(2))
+        forward_turned()
         for copy in grad_copies():
             copy.wait_recv()
         upper()
@@ -323,6 +373,13 @@
     @pl.when(first_seg)
     def _():
         start_all(dout_copies())
+
+    @pl.when(last_seg)
+    def _():
+        store_out.start()
+        start_all(turned_copies(1))
+        turn_act()
+        start_all(turned_copies(2))
 
     def tap_grads(block, carry):
         cols = pl.ds(pl.multiple_of(block * LANE, LANE), LANE)
@@ -384,12 +441,12 @@
     def _():
         copies = grad_copies()
         start_all(copies)
-        turn()
+        forward_turned()
         for copy in copies:
             copy.wait_send()
         start_all(dpre_copies())
-        start_all(turned_copies())
-
+
+    store_grad.start()
     for i in range(width // LANE):
         cols = slice(LANE * i, LANE * (i + 1))
         ebuf[cols, :] = gk[:, cols].T
@@ -397,36 +454,43 @@
         cols = slice(LANE * i, LANE * (i + 1))
         tbuf[cols, :] = jnp.broadcast_to(gg1[0:1, cols], (LANE, LANE)).T
 
-    for copy in dpre_copies() + turned_copies() + dout_copies():
-        copy.wait()
-    own_pre = dpre4[j]
-    rhs_one = jnp.concatenate([own_pre] + [dpre_r[d] for d in range(3)], axis=0)
-
-    def y_copy(buf, got, d, offset):
-        peer = (dy + d) % n_y
-        return remote(buf.at[peer], got.at[d - 1], sem_y, offset + d - 1, "dp", peer)
+    low, high = pl.ds(0, n_z // 2), pl.ds(n_z // 2, n_z // 2)
+    up, down, far = (dy + 1) % n_y, (dy + n_y - 1) % n_y, (dy + 2) % n_y
+
+    def y_far(buf, inner, base_sem):
+        return [
+            remote(buf.at[far, low], inner.at[0], sem_y, base_sem, "dp", up),
+            remote(buf.at[far, high], inner.at[1], sem_y, base_sem + 1, "dp", down),
+        ]
+
+    def y_direct(buf, got, base_sem):
+        return [
+            remote(buf.at[up, high], got.at[0, high], sem_y, base_sem + 2, "dp", up),
+            remote(buf.at[down, low], got.at[1, low], sem_y, base_sem + 3, "dp", down),
+        ]
+
+    def y_summed(buf, got, base_sem):
+        return [
+            remote(buf.at[up, low], got.at[0, low], sem_y, base_sem + 4, "dp", up),
+            remote(buf.at[down, high], got.at[1, high], sem_y, base_sem + 5, "dp", down),
+        ]
 
     def z_copy(buf, got, d, offset):
         peer = (z + d) % n_z
         return remote(buf.at[peer], got.at[d - 1], sem_z, offset + d - 1, "tm", peer * 4 + j)
 
-    y_order = list(range(1, n_y)) + [0]
     rows_one = model // n_y
     rows_two = width // n_y
-    for d in y_order:
-        peer = (dy + d) % n_y
-        start = pl.multiple_of(peer * rows_one, rows_one)
-        lhs = jnp.concatenate([n_t[i, pl.ds(start, rows_one), :] for i in range(4)], axis=1)
-        part = dot(lhs, rhs_one)
-        for i in range(n_z):
-            pa[peer, i] = part[48 * i : 48 * (i + 1)].astype(BF16)
-        if d:
-            y_copy(pa, ya, d, 0).start()
-
+
+    for copy in dout_copies() + [c for part in range(3) for c in turned_copies(part)[:1]]:
+        copy.wait()
+    for part in range(3):
+        turned_copies(part)[1].wait_send()
+        turned_copies(part, True)[0].wait()
     rhs_two = jnp.concatenate([dout4[j]] + [dout_r[d] for d in range(3)], axis=0)
     lane = lax.broadcasted_iota(jnp.int32, (24, LANE), 1)
-    for d in y_order:
-        peer = (dy + d) % n_y
+
+    def part_two(peer):
         start = pl.multiple_of(peer * rows_two, rows_two)
         lhs = jnp.concatenate([a_t[i, pl.ds(start, rows_two), :] for i in range(4)], axis=1)
         part = dot(lhs, rhs_two)
@@ -437,24 +501,55 @@
             extra = jnp.where(lane == 32, tbuf[pl.ds(at_t, 24), :], extra)
             extra = jnp.where(lane == 33, tbuf[pl.ds(at_t + 24, 24), :], extra)
             mine = part[24 * i : 24 * (i + 1)]
-            low = jnp.concatenate([mine[:, 256:], extra], axis=1)
-            pb[peer, i] = jnp.concatenate([mine[:, :256], low], axis=0).astype(BF16)
-        if d:
-            y_copy(pb, yb, d, n_y - 1).start()
-
-    for buf, got, q_buf, z_got, off_y, off_z in (
-        (pa, ya, qa, za, 0, 0),
-        (pb, yb, qb, zb, n_y - 1, n_z - 1),
-    ):
-        for d in range(1, n_y):
-            y_copy(buf, got, d, off_y).wait()
+            lower = jnp.concatenate([mine[:, 256:], extra], axis=1)
+            pb[peer, i] = jnp.concatenate([mine[:, :256], lower], axis=0).astype(BF16)
+
+    part_two(far)
+    start_all(y_far(pb, yb_in, 6))
+    part_two(up)
+    part_two(down)
+    start_all(y_direct(pb, yb, 6))
+    part_two(dy)
+
+    for copy in dpre_copies():
+        copy.wait()
+    rhs_one = jnp.concatenate([dpre4[j]] + [dpre_r[d] for d in range(3)], axis=0)
+
+    def part_one(peer):
+        start = pl.multiple_of(peer * rows_one, rows_one)
+        lhs = jnp.concatenate([n_t[i, pl.ds(start, rows_one), :] for i in range(4)], axis=1)
+        part = dot(lhs, rhs_one)
         for i in range(n_z):
-            total = buf[dy, i].astype(F32)
-            for d in range(n_y - 1):
-                total = total + got[d, i].astype(F32)
+            pa[peer, i] = part[48 * i : 48 * (i + 1)].astype(BF16)
+
+    def y_relay(buf, inner, got, base_sem):
+        for copy in y_far(buf, inner, base_sem):
+            copy.wait()
+        for i in range(n_z // 2):
+            k = n_z // 2 + i
+            buf[up, i] = (buf[up, i].astype(F32) + inner[0, i].astype(F32)).astype(BF16)
+            buf[down, k] = (buf[down, k].astype(F32) + inner[1, i].astype(F32)).astype(BF16)
+        start_all(y_summed(buf, got, base_sem))
+
+    def y_finish(buf, got, q_buf, z_got, base_sem, z_sem):
+        for copy in y_direct(buf, got, base_sem) + y_summed(buf, got, base_sem):
+            copy.wait()
+        for i in range(n_z):
+            total = buf[dy, i].astype(F32) + got[0, i].astype(F32) + got[1, i].astype(F32)
             q_buf[i] = total.astype(BF16)
         for d in range(1, n_z):
-            z_copy(q_buf, z_got, d, off_z).start()
+            z_copy(q_buf, z_got, d, z_sem).start()
+
+    part_one(far)
+    start_all(y_far(pa, ya_in, 0))
+    part_one(up)
+    part_one(down)
+    start_all(y_direct(pa, ya, 0))
+    y_relay(pb, yb_in, yb, 6)
+    part_one(dy)
+    y_relay(pa, ya_in, ya, 0)
+    y_finish(pb, yb, qb, zb, 6, n_z - 1)
+    y_finish(pa, ya, qa, za, 0, 0)
 
     fs[...] = jnp.zeros_like(fs)
     for d in range(1, n_z):
@@ -473,8 +568,10 @@
     extra = total[24:, LANE:]
     for i in range(4):
         fs[i, 16:22, :] = two[6 * i : 6 * (i + 1)]
-        for m in range(3):
-            fs[i, 24:32, LANE * m : LANE * (m + 1)] = extra[8 * m : 8 * (m + 1)]
+        fs[i, 24:30, 0:LANE] = extra[6 * i : 6 * (i + 1)]
+        for m in range(2):
+            at = 12 * (i % 2) + 6 * m
+            fs[i, 24:30, LANE * (m + 1) : LANE * (m + 2)] = extra[at : at + 6]
     copies = [remote(fs.at[peer_j(d)], fr.at[j], sem_f, d, "tm", group[d]) for d in range(3)]
     start_all(copies)
     fr[j] = fs[j]
@@ -483,11 +580,33 @@
     small = jnp.zeros((8, 3 * LANE), F32)
     for i in range(4):
         cols = slice(384 * i, 384 * (i + 1))
-        o_one[:, cols] = fr[i, 0:12, :]
-        o_two[:, cols] = fr[i, 16:22, :]
+        for row in range(12):
+            o_one[row, :, cols] = fr[i, row : row + 1, :]
+        for row in range(6):
+            o_two[row, :, cols] = fr[i, 16 + row : 17 + row, :]
         small = small + fr[i, 24:32, :]
-    for m in range(3):
-        o_small[8 * m : 8 * (m + 1), :] = small[:, LANE * m : LANE * (m + 1)]
+    for i in range(6):
+        o_kern[i] = small[i : i + 1, :TAPS]
+    fill = jnp.zeros((LANE - 8, LANE), F32)
+    turned = [
+        jnp.concatenate([small[:, LANE * m : LANE * (m + 1)], fill], axis=0).T for m in range(3)
+    ]
+    o_gain2[...] = turned[0][TAPS : TAPS + 1, :6]
+    for m in range(2):
+        pair = turned[m + 1][32:34, :6]
+        o_gain1[:, 6 * m : 6 * (m + 1)] = jnp.where(j < 2, pair[0:1], pair[1:2])
+    store_out.wait()
+    store_grad.wait()
+
+
+def hand_over(*refs):
+    n = (len(refs) - 1) // 2
+    sems = refs[-1]
+    copies = [pltpu.make_async_copy(refs[i], refs[n + i], sems.at[i]) for i in range(n)]
+    for copy in copies:
+        copy.start()
+    for copy in copies:
+        copy.wait()
 
 
 def per_device(inputs, lengths, w_first, kernel_w, gain_first, gain_second, w_second, grad_output):
@@ -507,6 +626,10 @@
     padded = (frames + 2 * HALO, width)
     third = (4, frames, 384)
     scratch = [
+        buf((model, 2 * width), BF16),
+        buf((width, model), BF16),
+        buf(wide, BF16),
+        buf(wide, BF16),
         buf(wide, BF16),
         buf(wide, BF16),
         buf(wide, F32),
@@ -539,33 +662,40 @@
         buf((model, LANE), F32),
         buf((n_y, n_z, 48, 384), BF16),
         buf((n_y, n_z, 48, 256), BF16),
-        buf((n_y - 1, n_z, 48, 384), BF16),
-        buf((n_y - 1, n_z, 48, 256), BF16),
+        buf((2, n_z // 2, 48, 384), BF16),
+        buf((2, n_z // 2, 48, 256), BF16),
+        buf((2, n_z, 48, 384), BF16),
+        buf((2, n_z, 48, 256), BF16),
         buf((n_z, 48, 384), BF16),
         buf((n_z, 48, 256), BF16),
         buf((n_z - 1, 48, 384), BF16),
         buf((n_z - 1, 48, 256), BF16),
         buf((4, 32, 384), F32),
         buf((4, 32, 384), F32),
+        pltpu.SemaphoreType.DMA((4,)),
         pltpu.SemaphoreType.DMA((2, 4)),
         pltpu.SemaphoreType.DMA((2, 2)),
         pltpu.SemaphoreType.DMA((2, 2)),
+        pltpu.SemaphoreType.DMA((2, 15)),
         pltpu.SemaphoreType.DMA((2, 12)),
-        pltpu.SemaphoreType.DMA((2, 2 * (n_y - 1))),
         pltpu.SemaphoreType.DMA((2, 2 * (n_z - 1))),
         pltpu.SemaphoreType.DMA((2, 3)),
     ]
-    out, grad, one, two, small = pl.pallas_call(
+    hbm = pl.BlockSpec(memory_space=pl.ANY)
+    shapes = (
+        jax.ShapeDtypeStruct(wide, BF16),
+        jax.ShapeDtypeStruct(wide, BF16),
+        jax.ShapeDtypeStruct((model // groups, 1, model), F32),
+        jax.ShapeDtypeStruct((width // groups, 1, model), F32),
+        jax.ShapeDtypeStruct((width // groups, 1, TAPS), F32),
+        jax.ShapeDtypeStruct((1, model // groups), F32),
+        jax.ShapeDtypeStruct((1, width // groups), F32),
+    )
+    results = pl.pallas_call(
         functools.partial(kernel, n_y, n_z, n_tm),
-        out_shape=(
-            jax.ShapeDtypeStruct(wide, BF16),
-            jax.ShapeDtypeStruct(wide, BF16),
-            jax.ShapeDtypeStruct((model // groups, model), F32),
-            jax.ShapeDtypeStruct((width // groups, model), F32),
-            jax.ShapeDtypeStruct((24, LANE), F32),
-        ),
-        in_specs=[pl.BlockSpec(memory_space=pltpu.SMEM)] + [vmem] * 7,
-        out_specs=(vmem,) * 5,
+        out_shape=shapes,
+        in_specs=[pl.BlockSpec(memory_space=pltpu.SMEM), vmem, vmem, hbm, hbm, vmem, vmem, vmem],
+        out_specs=(hbm, hbm) + (vmem,) * 5,
         scratch_shapes=scratch,
         compiler_params=pltpu.CompilerParams(
             collective_id=0, has_side_effects=True, vmem_limit_bytes=60 * 1024 * 1024
@@ -579,21 +709,26 @@
         grad_output[0],
         w_first[0],
         w_second[0],
-        kernel_w[0],
+        kernel_w.transpose(1, 0, 2),
         gain_first,
         gain_second,
     )
-    j = lax.axis_index("tm") % 4
-    mine = lax.dynamic_slice(small, (6 * j, 0), (6, LANE))
-    g_one = lax.dynamic_slice(small[:, 32:34].T.reshape(48), (12 * j,), (12,))
+    out, grad, one, two, taps, g_one, g_two = pl.pallas_call(
+        hand_over,
+        out_shape=shapes,
+        in_specs=[hbm] * 7,
+        out_specs=(hbm,) * 7,
+        scratch_shapes=[pltpu.SemaphoreType.DMA((7,))],
+        compiler_params=pltpu.CompilerParams(vmem_limit_bytes=60 * 1024 * 1024),
+    )(*results)
     return (
         out[None, None],
         grad[None, None],
-        one[None],
-        mine[:, :TAPS].T[None],
-        g_one[None],
-        mine[:, TAPS][None],
-        two[None],
+        one.transpose(1, 0, 2),
+        taps.transpose(1, 2, 0),
+        g_one,
+        g_two,
+        two.transpose(1, 0, 2),
     )
 
 

time: 132 us -> 129 us (0.977)
  the two profiles are of different devices: /device:TPU:7 before, /device:TPU:1 now
where the time goes in v2:
time: 129 us; the launch traced here: 128 us
  Pallas kernels  127 us (98%)
  between operations  1.29 us (1%)
    pallas_call x1, Pallas kernels, per_device(): pl.pallas_call(functools.partial(kernel, n_y, n_z, n_tm), out_shape=shape...  98.6 us
    pallas_call x1, Pallas kernels, per_device(): pl.pallas_call(hand_over, out_shape=shapes, in_specs=[hbm] * 7, out_specs...  28.5 us

profile of v2, /device:TPU:1, one launch (start us, length us, event | category | flops | bytes accessed | tf_op | source)
XLA Modules:
  0.0 128.4 jit_solution(5844077107915512023)
XLA Ops:
  1.3 98.6 %shard_map.135 = (bf16[128,1536]{1,0:T(8,128)(2,1)}, bf16[128,1536]{1,0:T(8,128)(2,1)}, f32[12,1,1536]{2,1,0:T(1,128)}, f32[6,1,1536]{2,1,0:T(1,128)}, f32[6,1,3...) custom-call(s32[1]{0:T(128)S(6)} %copy.15.len_ref, bf16[128,1536]{1,0:T(8,128)(2,1)} %bitcast.12, ...), custom_call_target="tpu_custom_call" | custom-call | flops 2717908992 | bytes 12000000 | tf_op jit(solution)/shard_map/pallas_call | solution.py:694
  99.9 28.5 %shard_map.136 = (bf16[128,1536]{1,0:T(8,128)(2,1)}, bf16[128,1536]{1,0:T(8,128)(2,1)}, f32[12,1,1536]{2,1,0:T(1,128)}, f32[6,1,1536]{2,1,0:T(1,128)}, f32[6,1,3...) custom-call(bf16[128,1536]{1,0:T(8,128)(2,1)} %get-tuple-element.21.refs_0_, ...), custom_call_target="tpu_custom_call" | custom-call | tf_op jit(solution)/shard_map/pallas_call | solution.py:716

commit v3 on v2

--- a/solution.py
+++ b/solution.py
@@ -600,13 +600,9 @@
 
 
 def hand_over(*refs):
-    n = (len(refs) - 1) // 2
-    sems = refs[-1]
-    copies = [pltpu.make_async_copy(refs[i], refs[n + i], sems.at[i]) for i in range(n)]
-    for copy in copies:
-        copy.start()
-    for copy in copies:
-        copy.wait()
+    n = len(refs) // 2
+    for i in range(n):
+        refs[n + i][...] = refs[i][...]
 
 
 def per_device(inputs, lengths, w_first, kernel_w, gain_first, gain_second, w_second, grad_output):
@@ -716,9 +712,8 @@
     out, grad, one, two, taps, g_one, g_two = pl.pallas_call(
         hand_over,
         out_shape=shapes,
-        in_specs=[hbm] * 7,
-        out_specs=(hbm,) * 7,
-        scratch_shapes=[pltpu.SemaphoreType.DMA((7,))],
+        in_specs=[vmem] * 7,
+        out_specs=(vmem,) * 7,
         compiler_params=pltpu.CompilerParams(vmem_limit_bytes=60 * 1024 * 1024),
     )(*results)
     return (

time: 129 us -> 102 us (0.79)
  Pallas kernels: 127 us -> 101 us
    pallas_call x1, Pallas kernels: 28.5 us -> 2.09 us  [per_device(): pl.pallas_call(hand_over, out_shape=shapes, in_specs=[vmem] * 7, out_spec...]
where the time goes in v3:
time: 102 us
  Pallas kernels  101 us (99%)
  between operations  1.29 us (1%)
    pallas_call x1, Pallas kernels, per_device(): pl.pallas_call(functools.partial(kernel, n_y, n_z, n_tm), out_shape=shape...  98.6 us
    pallas_call x1, Pallas kernels, per_device(): pl.pallas_call(hand_over, out_shape=shapes, in_specs=[vmem] * 7, out_spec...  2.09 us

profile of v3, /device:TPU:1, one launch (start us, length us, event | category | flops | bytes accessed | tf_op | source)
XLA Modules:
  0.0 102.0 jit_solution(14354334059660081272)
XLA Ops:
  1.3 98.6 %shard_map.135 = (bf16[128,1536]{1,0:T(8,128)(2,1)}, bf16[128,1536]{1,0:T(8,128)(2,1)}, f32[12,1,1536]{2,1,0:T(1,128)}, f32[6,1,1536]{2,1,0:T(1,128)}, f32[6,1,3...) custom-call(s32[1]{0:T(128)S(6)} %copy.15.len_ref, bf16[128,1536]{1,0:T(8,128)(2,1)} %bitcast.12, ...), custom_call_target="tpu_custom_call" | custom-call | flops 2717908992 | bytes 12000000 | tf_op jit(solution)/shard_map/pallas_call | solution.py:690
  99.9 2.1 %shard_map.136 = (bf16[128,1536]{1,0:T(8,128)(2,1)}, bf16[128,1536]{1,0:T(8,128)(2,1)}, f32[12,1,1536]{2,1,0:T(1,128)}, f32[6,1,1536]{2,1,0:T(1,128)}, f32[6,1,3...) custom-call(bf16[128,1536]{1,0:T(8,128)(2,1)} %get-tuple-element.21.refs_0_, ...), custom_call_target="tpu_custom_call" | custom-call | tf_op jit(solution)/shard_map/pallas_call | solution.py:712

commit v4 on v3

v4 whole, which is shorter than its diff:
```python
import functools

import jax
import jax.numpy as jnp
from jax import lax
from jax.experimental import pallas as pl
from jax.experimental.pallas import tpu as pltpu
from jax.sharding import PartitionSpec as P

EPS = 1e-05
F32 = jnp.float32
BF16 = jnp.bfloat16
MESH = pl.DeviceIdType.MESH
NT = (((1,), (1,)), ((), ()))
HALO = 16
TAPS = 31
LANE = 128
ROWS = 32
EDGES = ((0, 16), (112, 16))
MIDDLE = ((16, 48), (64, 48))
EVERY = EDGES + MIDDLE


def chunk_rows(chunk):
    return [(EVERY.index(part), pl.ds(*part)) for part in chunk]


def dot(a, b):
    return jnp.dot(a, b, preferred_element_type=F32)


def dot_t(a, b):
    return lax.dot_general(a, b, NT, preferred_element_type=F32)


def kernel(
    n_y,
    n_z,
    n_tm,
    len_ref,
    inp,
    gout,
    w1_hbm,
    w2_hbm,
    kern,
    gain1,
    gain2,
    out_hbm,
    grad_hbm,
    o_one,
    o_two,
    o_kern,
    o_gain1,
    o_gain2,
    w1,
    w2,
    out_ref,
    grad_ref,
    cur,
    e,
    xhat,
    rstd1,
    normed,
    p_buf,
    sig_buf,
    gpad,
    dpad,
    conv,
    zhat,
    rstd2,
    zn_buf,
    act,
    d_act,
    d_norm,
    edge_g,
    edge_d,
    halo_g,
    halo_d,
    dout4,
    dpre4,
    dout_r,
    dpre_r,
    n_raw,
    a_raw,
    n_t,
    a_t,
    gk,
    gg1,
    ebuf,
    tbuf,
    item_a,
    item_b,
    item_c,
    qy,
    y_got,
    fs,
    fr,
    sem_w,
    sem_h,
    sem_out,
    sem_grad,
    sem_x,
    sem_y,
    sem_z,
    sem_f,
):
    frames, model = inp.shape
    width = w2.shape[0]
    dy = lax.axis_index("dp")
    seg = lax.axis_index("segment")
    t = lax.axis_index("tm")
    c = t % 2
    xl = (t // 2) % 2
    z = t // 4
    j = t % 4
    base = z * 4
    group = [base + xl * 2 + (1 - c), base + (1 - xl) * 2 + c, base + (1 - xl) * 2 + (1 - c)]
    right = (t + 1) % n_tm
    left = (t + n_tm - 1) % n_tm
    first_seg = seg == 0
    last_seg = seg == 1

    def remote(src, dst, sems, index, axis, peer):
        return pltpu.make_async_remote_copy(
            src_ref=src,
            dst_ref=dst,
            send_sem=sems.at[0, index],
            recv_sem=sems.at[1, index],
            device_id={axis: peer},
            device_id_type=MESH,
        )

    load_w1 = pltpu.make_async_copy(w1_hbm, w1, sem_w.at[0])
    load_w2 = pltpu.make_async_copy(w2_hbm, w2, sem_w.at[1])
    store_out = pltpu.make_async_copy(out_ref, out_hbm, sem_w.at[2])
    store_grad = pltpu.make_async_copy(grad_ref, grad_hbm, sem_w.at[3])
    barrier = pltpu.get_barrier_semaphore()
    greet = [("tm", left), ("tm", right), ("segment", 1 - seg)]
    greet += [("tm", g) for g in group]
    greet += [("dp", (dy + d) % n_y) for d in range(1, n_y)]
    greet += [("tm", ((z + d) % n_z) * 4 + j) for d in (1, 2, n_z - 1, n_z - 2)]
    for axis, peer in greet:
        pl.semaphore_signal(barrier, inc=1, device_id={axis: peer}, device_id_type=MESH)

    @pl.when(first_seg)
    def _():
        load_w1.start()
        load_w2.start()

    @pl.when(last_seg)
    def _():
        load_w2.start()
        load_w1.start()

    length = len_ref[0]

    def mask_of(start, rows):
        ids = t * frames + start + lax.broadcasted_iota(jnp.int32, (rows, 1), 0)
        return (ids < length).astype(F32)

    def out_copies(chunk):
        return [
            remote(out_ref.at[rows], cur.at[rows], sem_out, i, "segment", 1 - seg)
            for i, rows in chunk_rows(chunk)
        ]

    def grad_copies(chunk):
        return [
            remote(grad_ref.at[rows], e.at[rows], sem_grad, i, "segment", 1 - seg)
            for i, rows in chunk_rows(chunk)
        ]

    def halo_copies(edge, halo, offset):
        return [
            remote(edge.at[0], halo.at[1], sem_h, offset, "tm", left),
            remote(edge.at[1], halo.at[0], sem_h, offset + 1, "tm", right),
        ]

    def peer_j(d):
        return group[d] % 4

    def dout_copies(chunk):
        return [
            remote(
                dout4.at[peer_j(d), rows], dout_r.at[d, rows], sem_x, 3 * i + d, "tm", group[d]
            )
            for i, rows in chunk_rows(chunk)
            for d in range(3)
        ]

    def dpre_copies():
        return [
            remote(dpre4.at[peer_j(d)], dpre_r.at[d], sem_x, 12 + d, "tm", group[d]) for d in range(3)
        ]

    def turned_copies(part, forward=False):
        own, got = (act, a_raw) if part == 2 else (normed, n_raw)
        rows = pl.ds(0, frames) if part == 2 else pl.ds(frames // 2 * part, frames // 2)

        def one(src, dst, d):
            return remote(
                src.at[rows], got.at[dst, rows], sem_x, 15 + 3 * part + d, "tm", group[d % 2]
            )

        return [one(got.at[1], 2, 2)] if forward else [one(own, 0, 0), one(own, 1, 1)]

    def forward_turned(parts):
        for part in parts:
            turned_copies(part)[1].wait_recv()
            turned_copies(part, True)[0].start()

    def wait_turned(parts):
        for part in parts:
            copies = turned_copies(part)
            copies[0].wait()
            copies[1].wait_send()
            turned_copies(part, True)[0].wait()

    def start_all(copies):
        for copy in copies:
            copy.start()

    def stacked(ref, chunk):
        return jnp.concatenate([ref[start : start + size] for start, size in chunk], axis=0)

    def spread(value, chunk):
        at = 0
        for start, size in chunk:
            yield slice(start, start + size), value[at : at + size]
            at += size

    def pieces(chunk):
        return [(at, min(ROWS, start + size - at)) for start, size in chunk for at in range(start, start + size, ROWS)]

    def upper(chunk):
        for start, size in pieces(chunk):
            rows = slice(start, start + size)
            d_out = (e[rows, :].astype(F32) * mask_of(start, size)).astype(BF16)
            for i in range(4):
                dout4[i, rows, :] = d_out[:, 384 * i : 384 * (i + 1)]
        d_out = jnp.concatenate([stacked(dout4.at[i], chunk) for i in range(4)], axis=1)
        for n in range(width // 256):
            cols = slice(256 * n, 256 * (n + 1))
            for rows, value in spread(dot_t(d_out, w2[cols, :]), chunk):
                d_act[rows, cols] = value

    def taps_over(src, block, flip):
        cols = pl.ds(pl.multiple_of(block * LANE, LANE), LANE)
        whole = src[:, cols]
        total = jnp.zeros((frames, LANE), F32)
        for r in range(8):
            moved = whole if r == 0 else pltpu.roll(whole, whole.shape[0] - r, 0)
            for k in range(TAPS):
                if (k + 1) % 8 == r:
                    at = k + 1 - r
                    tap = TAPS - 1 - k if flip else k
                    total = total + kern[tap, :, cols] * moved[at : at + frames]
        return cols, total

    def turn(slots):
        for slot in slots:
            n_src = normed if slot == 0 else n_raw.at[slot - 1]
            a_src = act if slot == 0 else a_raw.at[slot - 1]
            for i in range(model // LANE):
                cols = slice(LANE * i, LANE * (i + 1))
                n_t[slot, cols, :] = n_src[:, cols].T
            for i in range(width // LANE):
                cols = slice(LANE * i, LANE * (i + 1))
                a_t[slot, cols, :] = a_src[:, cols].T

    gg1[...] = jnp.zeros_like(gg1)
    gk[...] = jnp.zeros_like(gk)

    @pl.when(last_seg)
    def _():
        e[...] = gout[...]
        load_w2.wait()
        upper(EVERY)

    @pl.when(first_seg)
    def _():
        cur[...] = inp[...]

    pl.semaphore_wait(barrier, len(greet))

    @pl.when(last_seg)
    def _():
        start_all(dout_copies(EVERY))

    def front(chunk, edge):
        for start, size in pieces(chunk):
            rows = slice(start, start + size)
            x = cur[rows, :].astype(F32)
            centred = x - jnp.mean(x, axis=-1, keepdims=True)
            rstd = lax.rsqrt(jnp.mean(centred * centred, axis=-1, keepdims=True) + EPS)
            hat = centred * rstd
            xhat[rows, :] = hat
            rstd1[rows, :] = jnp.broadcast_to(rstd, (size, LANE))
            normed[rows, :] = (hat * gain1[...]).astype(BF16)
        x = stacked(normed, chunk)
        mask = jnp.concatenate([mask_of(start, size) for start, size in chunk], axis=0)
        for n in range(width // 256):
            cols = slice(256 * n, 256 * (n + 1))
            q_cols = slice(width + 256 * n, width + 256 * (n + 1))
            p = dot(x, w1[:, cols])
            sig = jax.nn.sigmoid(dot(x, w1[:, q_cols]))
            gated = (p * sig * mask).astype(BF16)
            for rows, value in spread(p, chunk):
                p_buf[rows, cols] = value
            for rows, value in spread(sig, chunk):
                sig_buf[rows, cols] = value
            for rows, value in spread(gated.astype(F32), chunk):
                gpad[HALO + rows.start : HALO + rows.stop, cols] = value
            if edge:
                edge_g[0, :, cols] = gated[:HALO]
                edge_g[1, :, cols] = gated[HALO:]

    @pl.when(last_seg)
    def _():
        for copy in out_copies(EDGES):
            copy.wait_recv()

    @pl.when(first_seg)
    def _():
        load_w1.wait()

    @pl.when(last_seg)
    def _():
        load_w1.wait()

    front(EDGES, True)
    copies = halo_copies(edge_g, halo_g, 0)
    start_all(copies)

    @pl.when(last_seg)
    def _():
        for copy in out_copies(MIDDLE):
            copy.wait_recv()

    front(MIDDLE, False)

    @pl.when(last_seg)
    def _():
        start_all(turned_copies(0))

    maskf = mask_of(0, frames)
    for copy in copies:
        copy.wait()
    has_left = (t > 0).astype(F32)
    has_right = (t < n_tm - 1).astype(F32)
    gpad[0:HALO, :] = halo_g[0].astype(F32) * has_left
    gpad[HALO + frames :, :] = halo_g[1].astype(F32) * has_right

    def conv_block(block, carry):
        cols, total = taps_over(gpad, block, False)
        conv[:, cols] = total
        return carry

    lax.fori_loop(0, width // LANE, conv_block, 0)

    def act_rows(chunk):
        for start, size in pieces(chunk):
            rows = slice(start, start + size)
            x = conv[rows, :]
            centred = x - jnp.mean(x, axis=-1, keepdims=True)
            rstd = lax.rsqrt(jnp.mean(centred * centred, axis=-1, keepdims=True) + EPS)
            hat = centred * rstd
            zn = hat * gain2[...]
            zhat[rows, :] = hat
            zn_buf[rows, :] = zn
            rstd2[rows, :] = jnp.broadcast_to(rstd, (size, LANE))
            act[rows, :] = (zn * jax.nn.sigmoid(zn)).astype(BF16)

    def out_rows(chunk):
        x = stacked(act, chunk)
        for n in range(model // 512):
            cols = slice(512 * n, 512 * (n + 1))
            for rows, value in spread(dot(x, w2[:, cols]), chunk):
                mask = mask_of(rows.start, rows.stop - rows.start)
                out_ref[rows, cols] = (cur[rows, cols].astype(F32) + mask * value).astype(BF16)

    @pl.when(first_seg)
    def _():
        load_w2.wait()
        for chunk in (EDGES, MIDDLE):
            act_rows(chunk)
            out_rows(chunk)
            start_all(out_copies(chunk))
        store_out.start()
        turn((0,))
        for copy in out_copies(EVERY):
            copy.wait_send()
        for part in range(3):
            start_all(turned_copies(part))
        forward_turned((0, 1, 2))
        wait_turned((0, 1, 2))
        turn((1, 2, 3))

    @pl.when(last_seg)
    def _():
        act_rows(EVERY)

    def conv_grad(chunk):
        for start, size in pieces(chunk):
            rows = slice(start, start + size)
            zn = zn_buf[rows, :]
            hat = zhat[rows, :]
            sg = jax.nn.sigmoid(zn)
            d_zn = d_act[rows, :] * (sg + zn * sg * (1.0 - sg))
            gk[TAPS : TAPS + 1, :] += jnp.sum(d_zn * hat, axis=0, keepdims=True)
            d_hat = d_zn * gain2[...]
            m_one = jnp.mean(d_hat, axis=-1, keepdims=True)
            m_two = jnp.mean(d_hat * hat, axis=-1, keepdims=True)
            d_conv = rstd2[rows, 0:1] * (d_hat - m_one - hat * m_two)
            dpad[HALO + start : HALO + start + size, :] = d_conv

    halos = halo_copies(edge_d, halo_d, 2)

    def send_edges():
        edge_d[0] = dpad[HALO : 2 * HALO, :].astype(BF16)
        edge_d[1] = dpad[frames : HALO + frames, :].astype(BF16)
        start_all(halos)

    @pl.when(first_seg)
    def _():
        for chunk in (EDGES, MIDDLE[:1], MIDDLE[1:]):
            for copy in grad_copies(chunk):
                copy.wait_recv()
            upper(chunk)
            conv_grad(chunk)
            if chunk is EDGES:
                send_edges()
            start_all(dout_copies(chunk))

    @pl.when(last_seg)
    def _():
        conv_grad(EDGES)
        send_edges()
        start_all(turned_copies(1))
        start_all(turned_copies(2))
        conv_grad(MIDDLE)

    for copy in halos:
        copy.wait()
    dpad[0:HALO, :] = halo_d[0].astype(F32) * has_left
    dpad[HALO + frames :, :] = halo_d[1].astype(F32) * has_right

    for half in range(2):

        def pre_block(block, carry):
            cols, total = taps_over(dpad, half * 3 + block, True)
            d_gated = total * maskf
            sig = sig_buf[:, cols]
            d_p = d_gated * sig
            d_q = d_p * p_buf[:, cols] * (1.0 - sig)
            part = pl.ds(pl.multiple_of(block * LANE, LANE), LANE)
            dpre4[half, :, part] = d_p.astype(BF16)
            dpre4[2 + half, :, part] = d_q.astype(BF16)
            return carry

        lax.fori_loop(0, 3, pre_block, 0)

    @pl.when(first_seg)
    def _():
        start_all(dpre_copies())

    def grad_rows(chunk):
        d_pre = jnp.concatenate([stacked(dpre4.at[i], chunk) for i in range(4)], axis=1)
        for n in range(model // 512):
            cols = slice(512 * n, 512 * (n + 1))
            for rows, value in spread(dot_t(d_pre, w1[cols, :]), chunk):
                d_norm[rows, cols] = value
        for start, size in pieces(chunk):
            rows = slice(start, start + size)
            d_normed = d_norm[rows, :]
            hat = xhat[rows, :]
            gg1[0:1, :] += jnp.sum(d_normed * hat, axis=0, keepdims=True)
            d_hat = d_normed * gain1[...]
            m_one = jnp.mean(d_hat, axis=-1, keepdims=True)
            m_two = jnp.mean(d_hat * hat, axis=-1, keepdims=True)
            d_h = rstd1[rows, 0:1] * (d_hat - m_one - hat * m_two)
            grad_ref[rows, :] = (e[rows, :].astype(F32) + d_h).astype(BF16)

    @pl.when(first_seg)
    def _():
        grad_rows(EVERY)
        store_grad.start()

    @pl.when(last_seg)
    def _():
        for chunk in (EDGES, MIDDLE):
            grad_rows(chunk)
            start_all(grad_copies(chunk))
        start_all(dpre_copies())
        store_grad.start()
        out_rows(EVERY)
        store_out.start()
        turn((0,))
        forward_turned((2, 0, 1))
        wait_turned((2, 0, 1))
        turn((1, 2, 3))
        for copy in grad_copies(EVERY):
            copy.wait_send()

    def tap_grads(block, carry):
        cols = pl.ds(pl.multiple_of(block * LANE, LANE), LANE)
        whole = gpad[:, cols]
        d_conv = dpad[HALO : HALO + frames, cols]
        for r in range(8):
            moved = whole if r == 0 else pltpu.roll(whole, whole.shape[0] - r, 0)
            for k in range(TAPS):
                if (k + 1) % 8 == r:
                    at = k + 1 - r
                    gk[k : k + 1, cols] = jnp.sum(
                        moved[at : at + frames] * d_conv, axis=0, keepdims=True
                    )
        return carry

    low, high = pl.ds(0, n_z // 2), pl.ds(n_z // 2, n_z // 2)
    up, down, far = (dy + 1) % n_y, (dy + n_y - 1) % n_y, (dy + 2) % n_y

    def y_far(buf, inner, base_sem):
        return [
            remote(buf.at[far, low], inner.at[0], sem_y, base_sem, "dp", up),
            remote(buf.at[far, high], inner.at[1], sem_y, base_sem + 1, "dp", down),
        ]

    def y_direct(buf, got, base_sem):
        return [
            remote(buf.at[up, high], got.at[0, high], sem_y, base_sem + 2, "dp", up),
            remote(buf.at[down, low], got.at[1, low], sem_y, base_sem + 3, "dp", down),
        ]

    def y_summed(buf, got, base_sem):
        return [
            remote(buf.at[up, low], got.at[0, low], sem_y, base_sem + 4, "dp", up),
            remote(buf.at[down, high], got.at[1, high], sem_y, base_sem + 5, "dp", down),
        ]

    def z_peer(d):
        return ((z + d + n_z) % n_z) * 4 + j

    def z_far(item):
        q_buf, in_three, in_four, _, base_sem = item[3:]
        parts = q_buf.shape[1] // 2
        copies = []
        for i, d in enumerate((1, -1)):
            over = pl.ds(parts * i, parts)
            three, four = (z + 3 * d + n_z) % n_z, (z + 4) % n_z
            to = z_peer(2 * d)
            at = base_sem + 2 * i
            copies.append(remote(q_buf.at[three], in_three.at[i], sem_z, at, "tm", to))
            copies.append(remote(q_buf.at[four, over], in_four.at[i], sem_z, at + 1, "tm", to))
        return copies

    def z_near(item):
        q_buf, _, _, got, base_sem = item[3:]
        copies = []
        for i, d in enumerate((2, -2, 1, -1)):
            peer = (z + d + n_z) % n_z
            at = base_sem + 4 + i
            copies.append(remote(q_buf.at[peer], got.at[i], sem_z, at, "tm", z_peer(d)))
        return copies

    def z_relay(item):
        q_buf, in_three, in_four, _, _ = item[3:]
        parts = q_buf.shape[1] // 2
        for copy in z_far(item):
            copy.wait()
        copies = z_near(item)
        for i, d in enumerate((2, -2)):
            peer = (z + d + n_z) % n_z
            for m in range(parts):
                k = parts * i + m
                q_buf[peer, k] = (q_buf[peer, k].astype(F32) + in_four[i, m].astype(F32)).astype(BF16)
            copies[i].start()
        for i, d in enumerate((1, -1)):
            peer = (z + d + n_z) % n_z
            q_buf[peer] = (q_buf[peer].astype(F32) + in_three[i].astype(F32)).astype(BF16)
            copies[2 + i].start()

    def z_total(item):
        q_buf, _, _, got, _ = item[3:]
        for copy in z_near(item):
            copy.wait()
        total = q_buf[z].astype(F32)
        for i in range(4):
            total = total + got[i].astype(F32)
        return total

    def b_copies():
        return [
            remote(qy.at[(dy + d) % n_y], y_got.at[d - 1], sem_y, 11 + d, "dp", (dy + d) % n_y)
            for d in range(1, n_y)
        ]

    rows_one = model // n_y
    rows_two = width // n_y

    for copy in dout_copies(EVERY):
        copy.wait()
    rhs_two = jnp.concatenate([dout4[j]] + [dout_r[d] for d in range(3)], axis=0)
    item_a = tuple(item_a) + (0,)
    item_b = (None,) * 3 + tuple(item_b) + (8,)
    item_c = tuple(item_c) + (16,)

    def product(turned, peer, rows, rhs):
        start = pl.multiple_of(peer * rows, rows)
        lhs = jnp.concatenate([turned[i, pl.ds(start, rows), :] for i in range(4)], axis=1)
        return dot(lhs, rhs)

    def part_two(peer):
        part = product(a_t, peer, rows_two, rhs_two)
        fill = jnp.zeros((8, LANE), F32)
        for i in range(n_z):
            mine = part[24 * i : 24 * (i + 1)]
            blocks = [mine[:, LANE * m : LANE * (m + 1)] for m in range(3)]
            item_b[3][i, peer] = jnp.concatenate(blocks + [fill], axis=0).astype(BF16)

    def part_one(peer):
        part = product(n_t, peer, rows_one, rhs_one[:, :256])
        for i in range(n_z):
            for m in range(2):
                mine = part[48 * i : 48 * (i + 1), LANE * m : LANE * (m + 1)]
                item_a[0][peer, i, m] = mine.astype(BF16)

    def part_last(peer):
        part = product(n_t, peer, rows_one, rhs_one[:, 256:])
        lane = lax.broadcasted_iota(jnp.int32, (24, LANE), 1)
        for i in range(n_z):
            at = pl.multiple_of(peer * rows_two + 24 * i, 8)
            at_t = pl.multiple_of(peer * rows_one + 48 * i, 8)
            extra = ebuf[pl.ds(at, 24), :]
            extra = jnp.where(lane == 32, tbuf[pl.ds(at_t, 24), :], extra)
            extra = jnp.where(lane == 33, tbuf[pl.ds(at_t + 24, 24), :], extra)
            top = extra[:8] + pltpu.roll(extra[8:16], 64, 1)
            item_c[0][peer, i, 0] = part[48 * i : 48 * i + 32].astype(BF16)
            blocks = [part[48 * i + 32 : 48 * (i + 1)], top, extra[16:]]
            item_c[0][peer, i, 1] = jnp.concatenate(blocks, axis=0).astype(BF16)

    def y_begin(item, fill, base_sem):
        buf, inner, got = item[:3]
        fill(far)
        start_all(y_far(buf, inner, base_sem))
        fill(up)
        fill(down)
        start_all(y_direct(buf, got, base_sem))
        fill(dy)

    def y_relay(item, base_sem):
        buf, inner, got = item[:3]
        for copy in y_far(buf, inner, base_sem):
            copy.wait()
        for i in range(n_z // 2):
            k = n_z // 2 + i
            buf[up, i] = (buf[up, i].astype(F32) + inner[0, i].astype(F32)).astype(BF16)
            buf[down, k] = (buf[down, k].astype(F32) + inner[1, i].astype(F32)).astype(BF16)
        start_all(y_summed(buf, got, base_sem))

    def y_finish(item, base_sem):
        buf, _, got, q_buf = item[:4]
        for copy in y_direct(buf, got, base_sem) + y_summed(buf, got, base_sem):
            copy.wait()

        def total(d):
            at = (z + d) % n_z
            mine = buf[dy, at].astype(F32) + got[0, at].astype(F32) + got[1, at].astype(F32)
            q_buf[at] = mine.astype(BF16)

        for d in (3, 5, 4):
            total(d)
        start_all(z_far(item))
        for d in (2, 6, 1, 7, 0):
            total(d)

    for yy in range(n_y):
        part_two(yy)
    start_all(z_far(item_b))
    lax.fori_loop(0, width // LANE, tap_grads, 0)
    for i in range(width // LANE):
        cols = slice(LANE * i, LANE * (i + 1))
        ebuf[cols, :] = gk[:, cols].T
    for i in range(model // LANE):
        cols = slice(LANE * i, LANE * (i + 1))
        tbuf[cols, :] = jnp.broadcast_to(gg1[0:1, cols], (LANE, LANE)).T


    for copy in dpre_copies():
        copy.wait()
    rhs_one = jnp.concatenate([dpre4[j]] + [dpre_r[d] for d in range(3)], axis=0)
    y_begin(item_a, part_one, 0)
    z_relay(item_b)
    y_begin(item_c, part_last, 6)
    y_relay(item_a, 0)
    y_relay(item_c, 6)
    qy[...] = z_total(item_b).astype(BF16)
    start_all(b_copies())
    y_finish(item_a, 0)
    y_finish(item_c, 6)
    z_relay(item_a)

    fs[...] = jnp.zeros_like(fs)
    for copy in b_copies():
        copy.wait()
    total = qy[dy].astype(F32)
    for d in range(n_y - 1):
        total = total + y_got[d].astype(F32)
    for i in range(4):
        for m in range(3):
            at = 24 * m + 6 * i
            fs[i, 16:22, LANE * m : LANE * (m + 1)] = total[at : at + 6]
    z_relay(item_c)
    total = z_total(item_a)
    for i in range(4):
        for m in range(2):
            fs[i, 0:12, LANE * m : LANE * (m + 1)] = total[m, 12 * i : 12 * (i + 1)]
    total = z_total(item_c)
    whole = jnp.concatenate([total[0], total[1, :16]], axis=0)
    top = total[1, 16:24]
    extra = jnp.concatenate([top, pltpu.roll(top, 64, 1), total[1, 24:]], axis=0)
    for i in range(4):
        fs[i, 0:12, 256:] = whole[12 * i : 12 * (i + 1)]
        fs[i, 24:30, 0:LANE] = extra[6 * i : 6 * (i + 1)]
        for m in range(2):
            at = 12 * (i % 2) + 6 * m
            fs[i, 24:30, LANE * (m + 1) : LANE * (m + 2)] = extra[at : at + 6]
    copies = [remote(fs.at[peer_j(d)], fr.at[j], sem_f, d, "tm", group[d]) for d in range(3)]
    start_all(copies)
    fr[j] = fs[j]
    for copy in copies:
        copy.wait()
    small = jnp.zeros((8, 3 * LANE), F32)
    for i in range(4):
        cols = slice(384 * i, 384 * (i + 1))
        for row in range(12):
            o_one[row, :, cols] = fr[i, row : row + 1, :]
        for row in range(6):
            o_two[row, :, cols] = fr[i, 16 + row : 17 + row, :]
        small = small + fr[i, 24:32, :]
    for i in range(6):
        o_kern[i] = small[i : i + 1, :TAPS]
    fill = jnp.zeros((LANE - 8, LANE), F32)
    turned = [
        jnp.concatenate([small[:, LANE * m : LANE * (m + 1)], fill], axis=0).T for m in range(3)
    ]
    o_gain2[...] = turned[0][TAPS : TAPS + 1, :6]
    for m in range(2):
        pair = turned[m + 1][32:34, :6]
        o_gain1[:, 6 * m : 6 * (m + 1)] = jnp.where(j < 2, pair[0:1], pair[1:2])
    store_out.wait()
    store_grad.wait()


def hand_over(*refs):
    n = len(refs) // 2
    for i in range(n):
        refs[n + i][...] = refs[i][...]


def per_device(inputs, lengths, w_first, kernel_w, gain_first, gain_second, w_second, grad_output):
    n_y = lax.axis_size("dp")
    n_tm = lax.axis_size("tm")
    n_z = n_tm // 4
    frames, model = inputs.shape[1:]
    width = w_second.shape[1]
    groups = n_y * n_tm
    vmem = pl.BlockSpec(memory_space=pltpu.VMEM)

    def buf(shape, dtype):
        return pltpu.VMEM(shape, dtype)

    def second(parts, rows):
        return (
            buf((n_z, parts, rows, LANE), BF16),
            buf((2, parts, rows, LANE), BF16),
            buf((2, parts // 2, rows, LANE), BF16),
            buf((4, parts, rows, LANE), BF16),
        )

    def reduced(rows):
        return (
            buf((n_y, n_z, 2, rows, LANE), BF16),
            buf((2, n_z // 2, 2, rows, LANE), BF16),
            buf((2, n_z, 2, rows, LANE), BF16),
        ) + second(2, rows)

    wide = (frames, model)
    thin = (frames, width)
    padded = (frames + 2 * HALO, width)
    third = (4, frames, 384)
    scratch = [
        buf((model, 2 * width), BF16),
        buf((width, model), BF16),
        buf(wide, BF16),
        buf(wide, BF16),
        buf(wide, BF16),
        buf(wide, BF16),
        buf(wide, F32),
        buf((frames, LANE), F32),
        buf(wide, BF16),
        buf(thin, F32),
        buf(thin, F32),
        buf(padded, F32),
        buf(padded, F32),
        buf(thin, F32),
        buf(thin, F32),
        buf((frames, LANE), F32),
        buf(thin, F32),
        buf(thin, BF16),
        buf(thin, F32),
        buf(wide, F32),
        buf((2, HALO, width), BF16),
        buf((2, HALO, width), BF16),
        buf((2, HALO, width), BF16),
        buf((2, HALO, width), BF16),
        buf(third, BF16),
        buf(third, BF16),
        buf((3, frames, 384), BF16),
        buf((3, frames, 384), BF16),
        buf((3,) + wide, BF16),
        buf((3,) + thin, BF16),
        buf((4, model, LANE), BF16),
        buf((4, width, LANE), BF16),
        buf((LANE, width), F32),
        buf((8, model), F32),
        buf((width, LANE), F32),
        buf((model, LANE), F32),
        reduced(48),
        second(4, 80),
        reduced(32),
        buf((n_y, 80, LANE), BF16),
        buf((n_y - 1, 80, LANE), BF16),
        buf((4, 32, 384), F32),
        buf((4, 32, 384), F32),
        pltpu.SemaphoreType.DMA((4,)),
        pltpu.SemaphoreType.DMA((2, 4)),
        pltpu.SemaphoreType.DMA((2, 4)),
        pltpu.SemaphoreType.DMA((2, 4)),
        pltpu.SemaphoreType.DMA((2, 24)),
        pltpu.SemaphoreType.DMA((2, 15)),
        pltpu.SemaphoreType.DMA((2, 24)),
        pltpu.SemaphoreType.DMA((2, 3)),
    ]
    hbm = pl.BlockSpec(memory_space=pl.ANY)
    shapes = (
        jax.ShapeDtypeStruct(wide, BF16),
        jax.ShapeDtypeStruct(wide, BF16),
        jax.ShapeDtypeStruct((model // groups, 1, model), F32),
        jax.ShapeDtypeStruct((width // groups, 1, model), F32),
        jax.ShapeDtypeStruct((width // groups, 1, TAPS), F32),
        jax.ShapeDtypeStruct((1, model // groups), F32),
        jax.ShapeDtypeStruct((1, width // groups), F32),
    )
    results = pl.pallas_call(
        functools.partial(kernel, n_y, n_z, n_tm),
        out_shape=shapes,
        in_specs=[pl.BlockSpec(memory_space=pltpu.SMEM), vmem, vmem, hbm, hbm, vmem, vmem, vmem],
        out_specs=(hbm, hbm) + (vmem,) * 5,
        scratch_shapes=scratch,
        compiler_params=pltpu.CompilerParams(
            collective_id=0, has_side_effects=True, vmem_limit_bytes=60 * 1024 * 1024
        ),
        cost_estimate=pl.CostEstimate(
            flops=2 * 3 * frames * model * 3 * width, bytes_accessed=12_000_000, transcendentals=0
        ),
    )(
        lengths,
        inputs[0],
        grad_output[0],
        w_first[0],
        w_second[0],
        kernel_w.transpose(1, 0, 2),
        gain_first,
        gain_second,
    )
    out, grad, one, two, taps, g_one, g_two = pl.pallas_call(
        hand_over,
        out_shape=shapes,
        in_specs=[vmem] * 7,
        out_specs=(vmem,) * 7,
        compiler_params=pltpu.CompilerParams(vmem_limit_bytes=60 * 1024 * 1024),
    )(*results)
    return (
        out[None, None],
        grad[None, None],
        one.transpose(1, 0, 2),
        taps.transpose(1, 2, 0),
        g_one,
        g_two,
        two.transpose(1, 0, 2),
    )


def solution(mesh):
    in_specs = (
        P("dp", "tm", None),
        P("dp"),
        P("segment", None, None),
        P("segment", None, None),
        P("segment", None),
        P("segment", None),
        P("segment", None, None),
        P("dp", "tm", None),
    )
    out_specs = (
        P("segment", "dp", "tm", None),
        P("segment", "dp", "tm", None),
        P("segment", ("dp", "tm"), None),
        P("segment", None, ("dp", "tm")),
        P("segment", ("dp", "tm")),
        P("segment", ("dp", "tm")),
        P("segment", ("dp", "tm"), None),
    )
    return jax.shard_map(
        per_device, mesh=mesh, in_specs=in_specs, out_specs=out_specs, check_vma=False
    )
```

time: 102 us -> 94 us (0.922)
  Pallas kernels: 101 us -> 92.6 us
    pallas_call x1, Pallas kernels: 98.6 us -> 90.5 us  [per_device(): pl.pallas_call(functools.partial(kernel, n_y, n_z, n_tm), out_shape=shape...]
where the time goes in v4:
time: 94 us; the launch traced here: 93.9 us
  Pallas kernels  92.6 us (99%)
  between operations  1.29 us (1%)
    pallas_call x1, Pallas kernels, per_device(): pl.pallas_call(functools.partial(kernel, n_y, n_z, n_tm), out_shape=shape...  90.5 us
    pallas_call x1, Pallas kernels, per_device(): pl.pallas_call(hand_over, out_shape=shapes, in_specs=[vmem] * 7, out_spec...  2.09 us

profile of v4, /device:TPU:1, one launch (start us, length us, event | category | flops | bytes accessed | tf_op | source)
XLA Modules:
  0.0 93.9 jit_solution(15506415839322274786)
XLA Ops:
  1.3 90.5 %shard_map.135 = (bf16[128,1536]{1,0:T(8,128)(2,1)}, bf16[128,1536]{1,0:T(8,128)(2,1)}, f32[12,1,1536]{2,1,0:T(1,128)}, f32[6,1,1536]{2,1,0:T(1,128)}, f32[6,1,3...) custom-call(s32[1]{0:T(128)S(6)} %copy.15.len_ref, bf16[128,1536]{1,0:T(8,128)(2,1)} %bitcast.12, ...), custom_call_target="tpu_custom_call" | custom-call | flops 2717908992 | bytes 12000000 | tf_op jit(solution)/shard_map/pallas_call | solution.py:854
  91.8 2.1 %shard_map.136 = (bf16[128,1536]{1,0:T(8,128)(2,1)}, bf16[128,1536]{1,0:T(8,128)(2,1)}, f32[12,1,1536]{2,1,0:T(1,128)}, f32[6,1,1536]{2,1,0:T(1,128)}, f32[6,1,3...) custom-call(bf16[128,1536]{1,0:T(8,128)(2,1)} %get-tuple-element.21.refs_0_, ...), custom_call_target="tpu_custom_call" | custom-call | tf_op jit(solution)/shard_map/pallas_call | solution.py:876

commit v5 on v4

--- a/solution.py
+++ b/solution.py
@@ -91,10 +91,14 @@
     item_a,
     item_b,
     item_c,
+    item_d,
     qy,
     y_got,
+    dqy,
+    d_got,
     fs,
-    fr,
+    f_out,
+    f_in,
     sem_w,
     sem_h,
     sem_out,
@@ -188,18 +192,27 @@
             for d in range(3)
         ]
 
-    def dpre_copies():
+    def dpre_copies(last):
+        cols = pl.ds(256, LANE) if last else pl.ds(0, 256)
         return [
-            remote(dpre4.at[peer_j(d)], dpre_r.at[d], sem_x, 12 + d, "tm", group[d]) for d in range(3)
+            remote(
+                dpre4.at[peer_j(d), :, cols],
+                dpre_r.at[d, :, cols],
+                sem_x,
+                12 + 3 * last + d,
+                "tm",
+                group[d],
+            )
+            for d in range(3)
         ]
 
     def turned_copies(part, forward=False):
-        own, got = (act, a_raw) if part == 2 else (normed, n_raw)
-        rows = pl.ds(0, frames) if part == 2 else pl.ds(frames // 2 * part, frames // 2)
+        own, got = (act, a_raw) if part > 3 else (normed, n_raw)
+        rows = pl.ds(64 * (part - 4), 64) if part > 3 else pl.ds(32 * part, 32)
 
         def one(src, dst, d):
             return remote(
-                src.at[rows], got.at[dst, rows], sem_x, 15 + 3 * part + d, "tm", group[d % 2]
+                src.at[rows], got.at[dst, rows], sem_x, 18 + 3 * part + d, "tm", group[d % 2]
             )
 
         return [one(got.at[1], 2, 2)] if forward else [one(own, 0, 0), one(own, 1, 1)]
@@ -257,16 +270,19 @@
                     total = total + kern[tap, :, cols] * moved[at : at + frames]
         return cols, total
 
-    def turn(slots):
+    def turn_normed(slots):
         for slot in slots:
-            n_src = normed if slot == 0 else n_raw.at[slot - 1]
-            a_src = act if slot == 0 else a_raw.at[slot - 1]
+            src = normed if slot == 0 else n_raw.at[slot - 1]
             for i in range(model // LANE):
                 cols = slice(LANE * i, LANE * (i + 1))
-                n_t[slot, cols, :] = n_src[:, cols].T
+                n_t[slot, cols, :] = src[:, cols].T
+
+    def turn_act(slots):
+        for slot in slots:
+            src = act if slot == 0 else a_raw.at[slot - 1]
             for i in range(width // LANE):
                 cols = slice(LANE * i, LANE * (i + 1))
-                a_t[slot, cols, :] = a_src[:, cols].T
+                a_t[slot, cols, :] = src[:, cols].T
 
     gg1[...] = jnp.zeros_like(gg1)
     gk[...] = jnp.zeros_like(gk)
@@ -387,17 +403,20 @@
             out_rows(chunk)
             start_all(out_copies(chunk))
         store_out.start()
-        turn((0,))
+        turn_normed((0,))
+        turn_act((0,))
         for copy in out_copies(EVERY):
             copy.wait_send()
-        for part in range(3):
+        for part in range(6):
             start_all(turned_copies(part))
-        forward_turned((0, 1, 2))
-        wait_turned((0, 1, 2))
-        turn((1, 2, 3))
-
-    @pl.when(last_seg)
-    def _():
+        forward_turned(range(6))
+        wait_turned(range(6))
+        turn_normed((1, 2, 3))
+        turn_act((1, 2, 3))
+
+    @pl.when(last_seg)
+    def _():
+        start_all(turned_copies(1))
         act_rows(EVERY)
 
     def conv_grad(chunk):
@@ -436,12 +455,15 @@
     def _():
         conv_grad(EDGES)
         send_edges()
-        start_all(turned_copies(1))
-        start_all(turned_copies(2))
         conv_grad(MIDDLE)
 
     for copy in halos:
         copy.wait()
+
+    @pl.when(last_seg)
+    def _():
+        start_all(turned_copies(2))
+
     dpad[0:HALO, :] = halo_d[0].astype(F32) * has_left
     dpad[HALO + frames :, :] = halo_d[1].astype(F32) * has_right
 
@@ -462,7 +484,7 @@
 
     @pl.when(first_seg)
     def _():
-        start_all(dpre_copies())
+        start_all(dpre_copies(0) + dpre_copies(1))
 
     def grad_rows(chunk):
         d_pre = jnp.concatenate([stacked(dpre4.at[i], chunk) for i in range(4)], axis=1)
@@ -481,24 +503,22 @@
             d_h = rstd1[rows, 0:1] * (d_hat - m_one - hat * m_two)
             grad_ref[rows, :] = (e[rows, :].astype(F32) + d_h).astype(BF16)
 
-    @pl.when(first_seg)
-    def _():
-        grad_rows(EVERY)
-        store_grad.start()
-
     @pl.when(last_seg)
     def _():
         for chunk in (EDGES, MIDDLE):
             grad_rows(chunk)
             start_all(grad_copies(chunk))
-        start_all(dpre_copies())
+        for part in (4, 5, 3):
+            start_all(turned_copies(part))
+        start_all(dpre_copies(0) + dpre_copies(1))
         store_grad.start()
         out_rows(EVERY)
         store_out.start()
-        turn((0,))
-        forward_turned((2, 0, 1))
-        wait_turned((2, 0, 1))
-        turn((1, 2, 3))
+        turn_act((0,))
+        turn_normed((0,))
+        forward_turned((0, 1, 2, 4, 5))
+        wait_turned((0, 1, 2, 4, 5))
+        turn_act((1, 2, 3))
         for copy in grad_copies(EVERY):
             copy.wait_send()
 
@@ -545,12 +565,13 @@
         parts = q_buf.shape[1] // 2
         copies = []
         for i, d in enumerate((1, -1)):
-            over = pl.ds(parts * i, parts)
+            over = pl.ds(parts * i, parts if i == 0 else q_buf.shape[1] - parts)
             three, four = (z + 3 * d + n_z) % n_z, (z + 4) % n_z
             to = z_peer(2 * d)
             at = base_sem + 2 * i
             copies.append(remote(q_buf.at[three], in_three.at[i], sem_z, at, "tm", to))
-            copies.append(remote(q_buf.at[four, over], in_four.at[i], sem_z, at + 1, "tm", to))
+            into = in_four.at[i, pl.ds(0, over.size)]
+            copies.append(remote(q_buf.at[four, over], into, sem_z, at + 1, "tm", to))
         return copies
 
     def z_near(item):
@@ -570,7 +591,7 @@
         copies = z_near(item)
         for i, d in enumerate((2, -2)):
             peer = (z + d + n_z) % n_z
-            for m in range(parts):
+            for m in range(parts if i == 0 else q_buf.shape[1] - parts):
                 k = parts * i + m
                 q_buf[peer, k] = (q_buf[peer, k].astype(F32) + in_four[i, m].astype(F32)).astype(BF16)
             copies[i].start()
@@ -588,11 +609,19 @@
             total = total + got[i].astype(F32)
         return total
 
-    def b_copies():
+    def last_copies(buf, got, base_sem):
         return [
-            remote(qy.at[(dy + d) % n_y], y_got.at[d - 1], sem_y, 11 + d, "dp", (dy + d) % n_y)
+            remote(buf.at[(dy + d) % n_y], got.at[d - 1], sem_y, base_sem + d, "dp", (dy + d) % n_y)
             for d in range(1, n_y)
         ]
+
+    def last_total(buf, got, base_sem):
+        for copy in last_copies(buf, got, base_sem):
+            copy.wait()
+        total = buf[dy].astype(F32)
+        for d in range(n_y - 1):
+            total = total + got[d].astype(F32)
+        return total
 
     rows_one = model // n_y
     rows_two = width // n_y
@@ -601,8 +630,11 @@
         copy.wait()
     rhs_two = jnp.concatenate([dout4[j]] + [dout_r[d] for d in range(3)], axis=0)
     item_a = tuple(item_a) + (0,)
-    item_b = (None,) * 3 + tuple(item_b) + (8,)
-    item_c = tuple(item_c) + (16,)
+    item_b = tuple(item_b) + (8,)
+    item_c = (None,) * 3 + tuple(item_c) + (16,)
+    item_d = (None,) * 3 + tuple(item_d) + (24,)
+    qy_c = (qy, y_got, 11)
+    qy_d = (dqy, d_got, 14)
 
     def product(turned, peer, rows, rhs):
         start = pl.multiple_of(peer * rows, rows)
@@ -615,28 +647,48 @@
         for i in range(n_z):
             mine = part[24 * i : 24 * (i + 1)]
             blocks = [mine[:, LANE * m : LANE * (m + 1)] for m in range(3)]
-            item_b[3][i, peer] = jnp.concatenate(blocks + [fill], axis=0).astype(BF16)
+            whole = jnp.concatenate(blocks + [fill], axis=0).astype(BF16)
+            for m in range(5):
+                item_b[0][peer, i, m] = whole[16 * m : 16 * (m + 1)]
 
     def part_one(peer):
-        part = product(n_t, peer, rows_one, rhs_one[:, :256])
+        part = product(n_t, peer, rows_one, rhs_one)
         for i in range(n_z):
             for m in range(2):
                 mine = part[48 * i : 48 * (i + 1), LANE * m : LANE * (m + 1)]
                 item_a[0][peer, i, m] = mine.astype(BF16)
 
-    def part_last(peer):
-        part = product(n_t, peer, rows_one, rhs_one[:, 256:])
+    def part_last(d):
+        peer = (z + d + n_z) % n_z
+        starts = [pl.multiple_of(rows_one * yy + 48 * peer, 16) for yy in range(n_y)]
+        lhs = jnp.concatenate(
+            [
+                jnp.concatenate([n_t[i, pl.ds(start, 48), :] for i in range(4)], axis=1)
+                for start in starts
+            ],
+            axis=0,
+        )
+        part = dot(lhs, rhs_last)
+        for yy in range(n_y):
+            item_c[3][peer, yy] = part[48 * yy : 48 * (yy + 1)].astype(BF16)
+
+    def part_small():
+        for i in range(width // LANE):
+            cols = slice(LANE * i, LANE * (i + 1))
+            ebuf[cols, :] = gk[:, cols].T
+        for i in range(model // LANE):
+            cols = slice(LANE * i, LANE * (i + 1))
+            tbuf[cols, :] = jnp.broadcast_to(gg1[0:1, cols], (LANE, LANE)).T
         lane = lax.broadcasted_iota(jnp.int32, (24, LANE), 1)
-        for i in range(n_z):
-            at = pl.multiple_of(peer * rows_two + 24 * i, 8)
-            at_t = pl.multiple_of(peer * rows_one + 48 * i, 8)
-            extra = ebuf[pl.ds(at, 24), :]
-            extra = jnp.where(lane == 32, tbuf[pl.ds(at_t, 24), :], extra)
-            extra = jnp.where(lane == 33, tbuf[pl.ds(at_t + 24, 24), :], extra)
-            top = extra[:8] + pltpu.roll(extra[8:16], 64, 1)
-            item_c[0][peer, i, 0] = part[48 * i : 48 * i + 32].astype(BF16)
-            blocks = [part[48 * i + 32 : 48 * (i + 1)], top, extra[16:]]
-            item_c[0][peer, i, 1] = jnp.concatenate(blocks, axis=0).astype(BF16)
+        for peer in range(n_y):
+            for i in range(n_z):
+                at = peer * rows_two + 24 * i
+                at_t = peer * rows_one + 48 * i
+                extra = ebuf[at : at + 24, :]
+                extra = jnp.where(lane == 32, tbuf[at_t : at_t + 24, :], extra)
+                extra = jnp.where(lane == 33, tbuf[at_t + 24 : at_t + 48, :], extra)
+                top = extra[:8] + pltpu.roll(extra[8:16], 64, 1)
+                item_d[3][i, peer] = jnp.concatenate([top, extra[16:]], axis=0).astype(BF16)
 
     def y_begin(item, fill, base_sem):
         buf, inner, got = item[:3]
@@ -673,70 +725,89 @@
         for d in (2, 6, 1, 7, 0):
             total(d)
 
-    for yy in range(n_y):
-        part_two(yy)
-    start_all(z_far(item_b))
+    y_begin(item_b, part_two, 6)
+
+    @pl.when(last_seg)
+    def _():
+        forward_turned((3,))
+        wait_turned((3,))
+        turn_normed((1, 2, 3))
+
+    for copy in dpre_copies(0):
+        copy.wait()
+    rhs_one = jnp.concatenate([dpre4[j, :, :256]] + [dpre_r[d, :, :256] for d in range(3)], axis=0)
+    part_one(far)
+    start_all(y_far(item_a[0], item_a[1], 0))
+    for copy in dpre_copies(1):
+        copy.wait()
+    rhs_last = jnp.concatenate([dpre4[j, :, 256:]] + [dpre_r[d, :, 256:] for d in range(3)], axis=0)
+    for d in (3, -3, 4):
+        part_last(d)
+    start_all(z_far(item_c))
+    part_one(up)
+    part_one(down)
+    y_relay(item_b, 6)
+    start_all(y_direct(item_a[0], item_a[2], 0))
+    part_one(dy)
+    for d in (1, -1, 2, -2, 0):
+        part_last(d)
     lax.fori_loop(0, width // LANE, tap_grads, 0)
-    for i in range(width // LANE):
-        cols = slice(LANE * i, LANE * (i + 1))
-        ebuf[cols, :] = gk[:, cols].T
-    for i in range(model // LANE):
-        cols = slice(LANE * i, LANE * (i + 1))
-        tbuf[cols, :] = jnp.broadcast_to(gg1[0:1, cols], (LANE, LANE)).T
-
-
-    for copy in dpre_copies():
-        copy.wait()
-    rhs_one = jnp.concatenate([dpre4[j]] + [dpre_r[d] for d in range(3)], axis=0)
-    y_begin(item_a, part_one, 0)
+
+    @pl.when(first_seg)
+    def _():
+        grad_rows(EVERY)
+        store_grad.start()
+
+    y_relay(item_a, 0)
+    z_relay(item_c)
+    y_finish(item_b, 6)
+    part_small()
+    start_all(z_far(item_d))
+    y_finish(item_a, 0)
+    qy[...] = z_total(item_c).astype(BF16)
+    start_all(last_copies(*qy_c))
     z_relay(item_b)
-    y_begin(item_c, part_last, 6)
-    y_relay(item_a, 0)
-    y_relay(item_c, 6)
-    qy[...] = z_total(item_b).astype(BF16)
-    start_all(b_copies())
-    y_finish(item_a, 0)
-    y_finish(item_c, 6)
+    z_relay(item_d)
     z_relay(item_a)
+    dqy[...] = z_total(item_d).astype(BF16)
+    start_all(last_copies(*qy_d))
 
     fs[...] = jnp.zeros_like(fs)
-    for copy in b_copies():
-        copy.wait()
-    total = qy[dy].astype(F32)
-    for d in range(n_y - 1):
-        total = total + y_got[d].astype(F32)
+    total = z_total(item_b)
+    total = jnp.concatenate([total[m] for m in range(5)], axis=0)
     for i in range(4):
         for m in range(3):
             at = 24 * m + 6 * i
             fs[i, 16:22, LANE * m : LANE * (m + 1)] = total[at : at + 6]
-    z_relay(item_c)
     total = z_total(item_a)
     for i in range(4):
         for m in range(2):
             fs[i, 0:12, LANE * m : LANE * (m + 1)] = total[m, 12 * i : 12 * (i + 1)]
-    total = z_total(item_c)
-    whole = jnp.concatenate([total[0], total[1, :16]], axis=0)
-    top = total[1, 16:24]
-    extra = jnp.concatenate([top, pltpu.roll(top, 64, 1), total[1, 24:]], axis=0)
+    small = last_total(*qy_d)
+    top = small[:8]
+    extra = jnp.concatenate([top, pltpu.roll(top, 64, 1), small[8:]], axis=0)
+    total = last_total(*qy_c)
     for i in range(4):
-        fs[i, 0:12, 256:] = whole[12 * i : 12 * (i + 1)]
+        fs[i, 0:12, 256:] = total[12 * i : 12 * (i + 1)]
         fs[i, 24:30, 0:LANE] = extra[6 * i : 6 * (i + 1)]
         for m in range(2):
             at = 12 * (i % 2) + 6 * m
             fs[i, 24:30, LANE * (m + 1) : LANE * (m + 2)] = extra[at : at + 6]
-    copies = [remote(fs.at[peer_j(d)], fr.at[j], sem_f, d, "tm", group[d]) for d in range(3)]
+    f_out[...] = fs[...].astype(BF16)
+    copies = [remote(f_out.at[peer_j(d)], f_in.at[j], sem_f, d, "tm", group[d]) for d in range(3)]
     start_all(copies)
-    fr[j] = fs[j]
+    f_in[j] = f_out[j]
     for copy in copies:
         copy.wait()
+    fs[...] = f_in[...].astype(F32)
     small = jnp.zeros((8, 3 * LANE), F32)
     for i in range(4):
         cols = slice(384 * i, 384 * (i + 1))
         for row in range(12):
-            o_one[row, :, cols] = fr[i, row : row + 1, :]
+            o_one[row, :, cols] = fs[i, row : row + 1, :]
         for row in range(6):
-            o_two[row, :, cols] = fr[i, 16 + row : 17 + row, :]
-        small = small + fr[i, 24:32, :]
+            o_two[row, :, cols] = fs[i, 16 + row : 17 + row, :]
+        small = small + fs[i, 24:32, :]
     for i in range(6):
         o_kern[i] = small[i : i + 1, :TAPS]
     fill = jnp.zeros((LANE - 8, LANE), F32)
@@ -773,16 +844,16 @@
         return (
             buf((n_z, parts, rows, LANE), BF16),
             buf((2, parts, rows, LANE), BF16),
-            buf((2, parts // 2, rows, LANE), BF16),
+            buf((2, parts - parts // 2, rows, LANE), BF16),
             buf((4, parts, rows, LANE), BF16),
         )
 
-    def reduced(rows):
+    def reduced(parts, rows):
         return (
-            buf((n_y, n_z, 2, rows, LANE), BF16),
-            buf((2, n_z // 2, 2, rows, LANE), BF16),
-            buf((2, n_z, 2, rows, LANE), BF16),
-        ) + second(2, rows)
+            buf((n_y, n_z, parts, rows, LANE), BF16),
+            buf((2, n_z // 2, parts, rows, LANE), BF16),
+            buf((2, n_z, parts, rows, LANE), BF16),
+        ) + second(parts, rows)
 
     wide = (frames, model)
     thin = (frames, width)
@@ -825,20 +896,24 @@
         buf((8, model), F32),
         buf((width, LANE), F32),
         buf((model, LANE), F32),
-        reduced(48),
-        second(4, 80),
-        reduced(32),
-        buf((n_y, 80, LANE), BF16),
-        buf((n_y - 1, 80, LANE), BF16),
+        reduced(2, 48),
+        reduced(5, 16),
+        second(4, 48),
+        second(4, 16),
+        buf((n_y, 48, LANE), BF16),
+        buf((n_y - 1, 48, LANE), BF16),
+        buf((n_y, 16, LANE), BF16),
+        buf((n_y - 1, 16, LANE), BF16),
         buf((4, 32, 384), F32),
-        buf((4, 32, 384), F32),
+        buf((4, 32, 384), BF16),
+        buf((4, 32, 384), BF16),
         pltpu.SemaphoreType.DMA((4,)),
         pltpu.SemaphoreType.DMA((2, 4)),
         pltpu.SemaphoreType.DMA((2, 4)),
         pltpu.SemaphoreType.DMA((2, 4)),
-        pltpu.SemaphoreType.DMA((2, 24)),
-        pltpu.SemaphoreType.DMA((2, 15)),
-        pltpu.SemaphoreType.DMA((2, 24)),
+        pltpu.SemaphoreType.DMA((2, 36)),
+        pltpu.SemaphoreType.DMA((2, 18)),
+        pltpu.SemaphoreType.DMA((2, 32)),
         pltpu.SemaphoreType.DMA((2, 3)),
     ]
     hbm = pl.BlockSpec(memory_space=pl.ANY)

time: 94 us -> 89.1 us (0.948)
  Pallas kernels: 92.6 us -> 87.7 us
    pallas_call x1, Pallas kernels: 90.5 us -> 85.6 us  [per_device(): pl.pallas_call(functools.partial(kernel, n_y, n_z, n_tm), out_shape=shape...]
where the time goes in v5:
time: 89.1 us; the launch traced here: 89 us
  Pallas kernels  87.7 us (98%)
  between operations  1.29 us (1%)
    pallas_call x1, Pallas kernels, per_device(): pl.pallas_call(functools.partial(kernel, n_y, n_z, n_tm), out_shape=shape...  85.6 us
    pallas_call x1, Pallas kernels, per_device(): pl.pallas_call(hand_over, out_shape=shapes, in_specs=[vmem] * 7, out_spec...  2.09 us

profile of v5, /device:TPU:1, one launch (start us, length us, event | category | flops | bytes accessed | tf_op | source)
XLA Modules:
  0.0 89.0 jit_solution(15418736421723399793)
XLA Ops:
  1.3 85.6 %shard_map.135 = (bf16[128,1536]{1,0:T(8,128)(2,1)}, bf16[128,1536]{1,0:T(8,128)(2,1)}, f32[12,1,1536]{2,1,0:T(1,128)}, f32[6,1,1536]{2,1,0:T(1,128)}, f32[6,1,3...) custom-call(s32[1]{0:T(128)S(6)} %copy.15.len_ref, bf16[128,1536]{1,0:T(8,128)(2,1)} %bitcast.12, ...), custom_call_target="tpu_custom_call" | custom-call | flops 2717908992 | bytes 12000000 | tf_op jit(solution)/shard_map/pallas_call | solution.py:929
  86.9 2.1 %shard_map.136 = (bf16[128,1536]{1,0:T(8,128)(2,1)}, bf16[128,1536]{1,0:T(8,128)(2,1)}, f32[12,1,1536]{2,1,0:T(1,128)}, f32[6,1,1536]{2,1,0:T(1,128)}, f32[6,1,3...) custom-call(bf16[128,1536]{1,0:T(8,128)(2,1)} %get-tuple-element.21.refs_0_, ...), custom_call_target="tpu_custom_call" | custom-call | tf_op jit(solution)/shard_map/pallas_call | solution.py:951

commit v6 on v5

--- a/solution.py
+++ b/solution.py
@@ -85,17 +85,13 @@
     n_t,
     a_t,
     gk,
-    gg1,
     ebuf,
     tbuf,
     item_a,
     item_b,
     item_c,
-    item_d,
     qy,
     y_got,
-    dqy,
-    d_got,
     fs,
     f_out,
     f_in,
@@ -284,7 +280,9 @@
                 cols = slice(LANE * i, LANE * (i + 1))
                 a_t[slot, cols, :] = src[:, cols].T
 
-    gg1[...] = jnp.zeros_like(gg1)
+    for i in range(model // LANE):
+        cols = slice(LANE * i, LANE * (i + 1))
+        tbuf[cols, :] = jnp.broadcast_to(1.0 / gain1[:, cols], (LANE, LANE)).T
     gk[...] = jnp.zeros_like(gk)
 
     @pl.when(last_seg)
@@ -496,7 +494,6 @@
             rows = slice(start, start + size)
             d_normed = d_norm[rows, :]
             hat = xhat[rows, :]
-            gg1[0:1, :] += jnp.sum(d_normed * hat, axis=0, keepdims=True)
             d_hat = d_normed * gain1[...]
             m_one = jnp.mean(d_hat, axis=-1, keepdims=True)
             m_two = jnp.mean(d_hat * hat, axis=-1, keepdims=True)
@@ -632,9 +629,7 @@
     item_a = tuple(item_a) + (0,)
     item_b = tuple(item_b) + (8,)
     item_c = (None,) * 3 + tuple(item_c) + (16,)
-    item_d = (None,) * 3 + tuple(item_d) + (24,)
     qy_c = (qy, y_got, 11)
-    qy_d = (dqy, d_got, 14)
 
     def product(turned, peer, rows, rhs):
         start = pl.multiple_of(peer * rows, rows)
@@ -643,10 +638,12 @@
 
     def part_two(peer):
         part = product(a_t, peer, rows_two, rhs_two)
-        fill = jnp.zeros((8, LANE), F32)
         for i in range(n_z):
             mine = part[24 * i : 24 * (i + 1)]
             blocks = [mine[:, LANE * m : LANE * (m + 1)] for m in range(3)]
+            at = pl.multiple_of(peer * rows_two + 24 * i, 8)
+            extra = ebuf[pl.ds(at, 24), :]
+            fill = extra[:8] + pltpu.roll(extra[8:16], 32, 1) + pltpu.roll(extra[16:], 64, 1)
             whole = jnp.concatenate(blocks + [fill], axis=0).astype(BF16)
             for m in range(5):
                 item_b[0][peer, i, m] = whole[16 * m : 16 * (m + 1)]
@@ -672,24 +669,6 @@
         for yy in range(n_y):
             item_c[3][peer, yy] = part[48 * yy : 48 * (yy + 1)].astype(BF16)
 
-    def part_small():
-        for i in range(width // LANE):
-            cols = slice(LANE * i, LANE * (i + 1))
-            ebuf[cols, :] = gk[:, cols].T
-        for i in range(model // LANE):
-            cols = slice(LANE * i, LANE * (i + 1))
-            tbuf[cols, :] = jnp.broadcast_to(gg1[0:1, cols], (LANE, LANE)).T
-        lane = lax.broadcasted_iota(jnp.int32, (24, LANE), 1)
-        for peer in range(n_y):
-            for i in range(n_z):
-                at = peer * rows_two + 24 * i
-                at_t = peer * rows_one + 48 * i
-                extra = ebuf[at : at + 24, :]
-                extra = jnp.where(lane == 32, tbuf[at_t : at_t + 24, :], extra)
-                extra = jnp.where(lane == 33, tbuf[at_t + 24 : at_t + 48, :], extra)
-                top = extra[:8] + pltpu.roll(extra[8:16], 64, 1)
-                item_d[3][i, peer] = jnp.concatenate([top, extra[16:]], axis=0).astype(BF16)
-
     def y_begin(item, fill, base_sem):
         buf, inner, got = item[:3]
         fill(far)
@@ -725,6 +704,10 @@
         for d in (2, 6, 1, 7, 0):
             total(d)
 
+    lax.fori_loop(0, width // LANE, tap_grads, 0)
+    for i in range(width // LANE):
+        cols = slice(LANE * i, LANE * (i + 1))
+        ebuf[cols, :] = gk[:, cols].T
     y_begin(item_b, part_two, 6)
 
     @pl.when(last_seg)
@@ -751,7 +734,6 @@
     part_one(dy)
     for d in (1, -1, 2, -2, 0):
         part_last(d)
-    lax.fori_loop(0, width // LANE, tap_grads, 0)
 
     @pl.when(first_seg)
     def _():
@@ -761,16 +743,11 @@
     y_relay(item_a, 0)
     z_relay(item_c)
     y_finish(item_b, 6)
-    part_small()
-    start_all(z_far(item_d))
     y_finish(item_a, 0)
     qy[...] = z_total(item_c).astype(BF16)
     start_all(last_copies(*qy_c))
     z_relay(item_b)
-    z_relay(item_d)
     z_relay(item_a)
-    dqy[...] = z_total(item_d).astype(BF16)
-    start_all(last_copies(*qy_d))
 
     fs[...] = jnp.zeros_like(fs)
     total = z_total(item_b)
@@ -779,20 +756,24 @@
         for m in range(3):
             at = 24 * m + 6 * i
             fs[i, 16:22, LANE * m : LANE * (m + 1)] = total[at : at + 6]
+    fill = total[72:]
+    extra = jnp.concatenate([fill, pltpu.roll(fill, 96, 1), pltpu.roll(fill, 64, 1)], axis=0)
+    for i in range(4):
+        fs[i, 24:30, 0:LANE] = extra[6 * i : 6 * (i + 1)]
     total = z_total(item_a)
     for i in range(4):
         for m in range(2):
             fs[i, 0:12, LANE * m : LANE * (m + 1)] = total[m, 12 * i : 12 * (i + 1)]
-    small = last_total(*qy_d)
-    top = small[:8]
-    extra = jnp.concatenate([top, pltpu.roll(top, 64, 1), small[8:]], axis=0)
-    total = last_total(*qy_c)
+    final = last_total(*qy_c)
+    mine = jnp.concatenate([total[0], total[1], final], axis=1)
+    place = pl.ds(pl.multiple_of((dy * n_z + z) * 48, 16), 48)
+    weights = w1[place, pl.ds(pl.multiple_of(j * 384, LANE), 384)].astype(F32)
+    gains = jnp.sum(mine * weights, axis=-1, keepdims=True) * tbuf[place, :]
     for i in range(4):
-        fs[i, 0:12, 256:] = total[12 * i : 12 * (i + 1)]
-        fs[i, 24:30, 0:LANE] = extra[6 * i : 6 * (i + 1)]
+        fs[i, 0:12, 256:] = final[12 * i : 12 * (i + 1)]
         for m in range(2):
-            at = 12 * (i % 2) + 6 * m
-            fs[i, 24:30, LANE * (m + 1) : LANE * (m + 2)] = extra[at : at + 6]
+            at = 12 * i + 6 * m
+            fs[i, 24:30, LANE * (m + 1) : LANE * (m + 2)] = gains[at : at + 6]
     f_out[...] = fs[...].astype(BF16)
     copies = [remote(f_out.at[peer_j(d)], f_in.at[j], sem_f, d, "tm", group[d]) for d in range(3)]
     start_all(copies)
@@ -816,8 +797,7 @@
     ]
     o_gain2[...] = turned[0][TAPS : TAPS + 1, :6]
     for m in range(2):
-        pair = turned[m + 1][32:34, :6]
-        o_gain1[:, 6 * m : 6 * (m + 1)] = jnp.where(j < 2, pair[0:1], pair[1:2])
+        o_gain1[:, 6 * m : 6 * (m + 1)] = turned[m + 1][0:1, :6]
     store_out.wait()
     store_grad.wait()
 
@@ -893,17 +873,13 @@
         buf((4, model, LANE), BF16),
         buf((4, width, LANE), BF16),
         buf((LANE, width), F32),
-        buf((8, model), F32),
         buf((width, LANE), F32),
         buf((model, LANE), F32),
         reduced(2, 48),
         reduced(5, 16),
         second(4, 48),
-        second(4, 16),
         buf((n_y, 48, LANE), BF16),
         buf((n_y - 1, 48, LANE), BF16),
-        buf((n_y, 16, LANE), BF16),
-        buf((n_y - 1, 16, LANE), BF16),
         buf((4, 32, 384), F32),
         buf((4, 32, 384), BF16),
         buf((4, 32, 384), BF16),
@@ -912,8 +888,8 @@
         pltpu.SemaphoreType.DMA((2, 4)),
         pltpu.SemaphoreType.DMA((2, 4)),
         pltpu.SemaphoreType.DMA((2, 36)),
-        pltpu.SemaphoreType.DMA((2, 18)),
-        pltpu.SemaphoreType.DMA((2, 32)),
+        pltpu.SemaphoreType.DMA((2, 15)),
+        pltpu.SemaphoreType.DMA((2, 24)),
         pltpu.SemaphoreType.DMA((2, 3)),
     ]
     hbm = pl.BlockSpec(memory_space=pl.ANY)

time: 89.1 us -> 86.3 us (0.969)
  Pallas kernels: 87.7 us -> 84.9 us
    pallas_call x1, Pallas kernels: 85.6 us -> 82.8 us  [per_device(): pl.pallas_call(functools.partial(kernel, n_y, n_z, n_tm), out_shape=shape...]
where the time goes in v6:
time: 86.3 us; the launch traced here: 86.2 us
  Pallas kernels  84.9 us (98%)
  between operations  1.29 us (1%)
    pallas_call x1, Pallas kernels, per_device(): pl.pallas_call(functools.partial(kernel, n_y, n_z, n_tm), out_shape=shape...  82.8 us
    pallas_call x1, Pallas kernels, per_device(): pl.pallas_call(hand_over, out_shape=shapes, in_specs=[vmem] * 7, out_spec...  2.09 us

profile of v6, /device:TPU:1, one launch (start us, length us, event | category | flops | bytes accessed | tf_op | source)
XLA Modules:
  0.0 86.2 jit_solution(11658793264817991017)
XLA Ops:
  1.3 82.8 %shard_map.135 = (bf16[128,1536]{1,0:T(8,128)(2,1)}, bf16[128,1536]{1,0:T(8,128)(2,1)}, f32[12,1,1536]{2,1,0:T(1,128)}, f32[6,1,1536]{2,1,0:T(1,128)}, f32[6,1,3...) custom-call(s32[1]{0:T(128)S(6)} %copy.15.len_ref, bf16[128,1536]{1,0:T(8,128)(2,1)} %bitcast.12, ...), custom_call_target="tpu_custom_call" | custom-call | flops 2717908992 | bytes 12000000 | tf_op jit(solution)/shard_map/pallas_call | solution.py:905
  84.1 2.1 %shard_map.136 = (bf16[128,1536]{1,0:T(8,128)(2,1)}, bf16[128,1536]{1,0:T(8,128)(2,1)}, f32[12,1,1536]{2,1,0:T(1,128)}, f32[6,1,1536]{2,1,0:T(1,128)}, f32[6,1,3...) custom-call(bf16[128,1536]{1,0:T(8,128)(2,1)} %get-tuple-element.21.refs_0_, ...), custom_call_target="tpu_custom_call" | custom-call | tf_op jit(solution)/shard_map/pallas_call | solution.py:927

commit v7 on v6

--- a/solution.py
+++ b/solution.py
@@ -291,16 +291,6 @@
         load_w2.wait()
         upper(EVERY)
 
-    @pl.when(first_seg)
-    def _():
-        cur[...] = inp[...]
-
-    pl.semaphore_wait(barrier, len(greet))
-
-    @pl.when(last_seg)
-    def _():
-        start_all(dout_copies(EVERY))
-
     def front(chunk, edge):
         for start, size in pieces(chunk):
             rows = slice(start, start + size)
@@ -329,32 +319,35 @@
                 edge_g[0, :, cols] = gated[:HALO]
                 edge_g[1, :, cols] = gated[HALO:]
 
+    @pl.when(first_seg)
+    def _():
+        cur[...] = inp[...]
+        load_w1.wait()
+        front(EDGES, True)
+
+    pl.semaphore_wait(barrier, len(greet))
+
     @pl.when(last_seg)
     def _():
+        start_all(dout_copies(EVERY))
+        load_w1.wait()
         for copy in out_copies(EDGES):
             copy.wait_recv()
-
-    @pl.when(first_seg)
-    def _():
-        load_w1.wait()
-
-    @pl.when(last_seg)
-    def _():
-        load_w1.wait()
-
-    front(EDGES, True)
+        front(EDGES, True)
+
     copies = halo_copies(edge_g, halo_g, 0)
     start_all(copies)
 
+    @pl.when(first_seg)
+    def _():
+        front(MIDDLE, False)
+
     @pl.when(last_seg)
     def _():
-        for copy in out_copies(MIDDLE):
-            copy.wait_recv()
-
-    front(MIDDLE, False)
-
-    @pl.when(last_seg)
-    def _():
+        for chunk in (MIDDLE[:1], MIDDLE[1:]):
+            for copy in out_copies(chunk):
+                copy.wait_recv()
+            front(chunk, False)
         start_all(turned_copies(0))
 
     maskf = mask_of(0, frames)
@@ -431,6 +424,20 @@
             d_conv = rstd2[rows, 0:1] * (d_hat - m_one - hat * m_two)
             dpad[HALO + start : HALO + start + size, :] = d_conv
 
+    def tap_grads(block, carry):
+        cols = pl.ds(pl.multiple_of(block * LANE, LANE), LANE)
+        whole = gpad[:, cols]
+        d_conv = dpad[HALO : HALO + frames, cols]
+        for r in range(8):
+            moved = whole if r == 0 else pltpu.roll(whole, whole.shape[0] - r, 0)
+            for k in range(TAPS):
+                if (k + 1) % 8 == r:
+                    at = k + 1 - r
+                    gk[k : k + 1, cols] = jnp.sum(
+                        moved[at : at + frames] * d_conv, axis=0, keepdims=True
+                    )
+        return carry
+
     halos = halo_copies(edge_d, halo_d, 2)
 
     def send_edges():
@@ -454,6 +461,7 @@
         conv_grad(EDGES)
         send_edges()
         conv_grad(MIDDLE)
+        lax.fori_loop(0, width // LANE, tap_grads, 0)
 
     for copy in halos:
         copy.wait()
@@ -465,24 +473,33 @@
     dpad[0:HALO, :] = halo_d[0].astype(F32) * has_left
     dpad[HALO + frames :, :] = halo_d[1].astype(F32) * has_right
 
-    for half in range(2):
-
-        def pre_block(block, carry):
-            cols, total = taps_over(dpad, half * 3 + block, True)
-            d_gated = total * maskf
-            sig = sig_buf[:, cols]
-            d_p = d_gated * sig
-            d_q = d_p * p_buf[:, cols] * (1.0 - sig)
-            part = pl.ds(pl.multiple_of(block * LANE, LANE), LANE)
-            dpre4[half, :, part] = d_p.astype(BF16)
-            dpre4[2 + half, :, part] = d_q.astype(BF16)
-            return carry
-
-        lax.fori_loop(0, 3, pre_block, 0)
+    def pre_blocks(first, last):
+        for half in range(2):
+
+            def pre_block(block, carry):
+                cols, total = taps_over(dpad, half * 3 + block, True)
+                d_gated = total * maskf
+                sig = sig_buf[:, cols]
+                d_p = d_gated * sig
+                d_q = d_p * p_buf[:, cols] * (1.0 - sig)
+                part = pl.ds(pl.multiple_of(block * LANE, LANE), LANE)
+                dpre4[half, :, part] = d_p.astype(BF16)
+                dpre4[2 + half, :, part] = d_q.astype(BF16)
+                return carry
+
+            lax.fori_loop(first, last, pre_block, 0)
+
+    pre_blocks(0, 2)
 
     @pl.when(first_seg)
     def _():
-        start_all(dpre_copies(0) + dpre_copies(1))
+        start_all(dpre_copies(0))
+
+    pre_blocks(2, 3)
+
+    @pl.when(first_seg)
+    def _():
+        start_all(dpre_copies(1))
 
     def grad_rows(chunk):
         d_pre = jnp.concatenate([stacked(dpre4.at[i], chunk) for i in range(4)], axis=1)
@@ -519,20 +536,6 @@
         for copy in grad_copies(EVERY):
             copy.wait_send()
 
-    def tap_grads(block, carry):
-        cols = pl.ds(pl.multiple_of(block * LANE, LANE), LANE)
-        whole = gpad[:, cols]
-        d_conv = dpad[HALO : HALO + frames, cols]
-        for r in range(8):
-            moved = whole if r == 0 else pltpu.roll(whole, whole.shape[0] - r, 0)
-            for k in range(TAPS):
-                if (k + 1) % 8 == r:
-                    at = k + 1 - r
-                    gk[k : k + 1, cols] = jnp.sum(
-                        moved[at : at + frames] * d_conv, axis=0, keepdims=True
-                    )
-        return carry
-
     low, high = pl.ds(0, n_z // 2), pl.ds(n_z // 2, n_z // 2)
     up, down, far = (dy + 1) % n_y, (dy + n_y - 1) % n_y, (dy + 2) % n_y
 
@@ -704,7 +707,10 @@
         for d in (2, 6, 1, 7, 0):
             total(d)
 
-    lax.fori_loop(0, width // LANE, tap_grads, 0)
+    @pl.when(first_seg)
+    def _():
+        lax.fori_loop(0, width // LANE, tap_grads, 0)
+
     for i in range(width // LANE):
         cols = slice(LANE * i, LANE * (i + 1))
         ebuf[cols, :] = gk[:, cols].T

time: 86.3 us -> 85.6 us (level)
  no operation moved by 1% of the time
where the time goes in v7:
time: 85.6 us; the launch traced here: 85.5 us
  Pallas kernels  84.2 us (98%)
  between operations  1.29 us (2%)
    pallas_call x1, Pallas kernels, per_device(): pl.pallas_call(functools.partial(kernel, n_y, n_z, n_tm), out_shape=shape...  82.1 us
    pallas_call x1, Pallas kernels, per_device(): pl.pallas_call(hand_over, out_shape=shapes, in_specs=[vmem] * 7, out_spec...  2.09 us

profile of v7, /device:TPU:1, one launch (start us, length us, event | category | flops | bytes accessed | tf_op | source)
XLA Modules:
  0.0 85.5 jit_solution(16906011998990167402)
XLA Ops:
  1.3 82.1 %shard_map.135 = (bf16[128,1536]{1,0:T(8,128)(2,1)}, bf16[128,1536]{1,0:T(8,128)(2,1)}, f32[12,1,1536]{2,1,0:T(1,128)}, f32[6,1,1536]{2,1,0:T(1,128)}, f32[6,1,3...) custom-call(s32[1]{0:T(128)S(6)} %copy.15.len_ref, bf16[128,1536]{1,0:T(8,128)(2,1)} %bitcast.12, ...), custom_call_target="tpu_custom_call" | custom-call | flops 2717908992 | bytes 12000000 | tf_op jit(solution)/shard_map/pallas_call | solution.py:911
  83.4 2.1 %shard_map.136 = (bf16[128,1536]{1,0:T(8,128)(2,1)}, bf16[128,1536]{1,0:T(8,128)(2,1)}, f32[12,1,1536]{2,1,0:T(1,128)}, f32[6,1,1536]{2,1,0:T(1,128)}, f32[6,1,3...) custom-call(bf16[128,1536]{1,0:T(8,128)(2,1)} %get-tuple-element.21.refs_0_, ...), custom_call_target="tpu_custom_call" | custom-call | tf_op jit(solution)/shard_map/pallas_call | solution.py:933

commit v8 on v7

--- a/solution.py
+++ b/solution.py
@@ -741,15 +741,16 @@
     for d in (1, -1, 2, -2, 0):
         part_last(d)
 
+    z_relay(item_c)
+    y_relay(item_a, 0)
+    y_finish(item_b, 6)
+    y_finish(item_a, 0)
+
     @pl.when(first_seg)
     def _():
         grad_rows(EVERY)
         store_grad.start()
 
-    y_relay(item_a, 0)
-    z_relay(item_c)
-    y_finish(item_b, 6)
-    y_finish(item_a, 0)
     qy[...] = z_total(item_c).astype(BF16)
     start_all(last_copies(*qy_c))
     z_relay(item_b)
@@ -809,9 +810,17 @@
 
 
 def hand_over(*refs):
-    n = len(refs) // 2
+    n = (len(refs) - 1) // 3
+    sources, results, held, sems = refs[:n], refs[n : 2 * n], refs[2 * n : 3 * n], refs[-1]
+    inward = [pltpu.make_async_copy(sources[i], held[i], sems.at[0, i]) for i in range(n)]
+    outward = [pltpu.make_async_copy(held[i], results[i], sems.at[1, i]) for i in range(n)]
+    for copy in inward:
+        copy.start()
     for i in range(n):
-        refs[n + i][...] = refs[i][...]
+        inward[i].wait()
+        outward[i].start()
+    for copy in outward:
+        copy.wait()
 
 
 def per_device(inputs, lengths, w_first, kernel_w, gain_first, gain_second, w_second, grad_output):
@@ -933,8 +942,10 @@
     out, grad, one, two, taps, g_one, g_two = pl.pallas_call(
         hand_over,
         out_shape=shapes,
-        in_specs=[vmem] * 7,
-        out_specs=(vmem,) * 7,
+        in_specs=[hbm] * 7,
+        out_specs=(hbm,) * 7,
+        scratch_shapes=[buf(shape.shape, shape.dtype) for shape in shapes]
+        + [pltpu.SemaphoreType.DMA((2, 7))],
         compiler_params=pltpu.CompilerParams(vmem_limit_bytes=60 * 1024 * 1024),
     )(*results)
     return (

time: 85.6 us -> 85.7 us (level)
  no operation moved by 1% of the time
where the time goes in v8:
time: 85.7 us; the launch traced here: 85.6 us
  Pallas kernels  84.2 us (98%)
  between operations  1.45 us (2%)
    pallas_call x1, Pallas kernels, per_device(): pl.pallas_call(functools.partial(kernel, n_y, n_z, n_tm), out_shape=shape...  82.1 us
    pallas_call x1, Pallas kernels, per_device(): pl.pallas_call(hand_over, out_shape=shapes, in_specs=[hbm] * 7, out_specs...  2.03 us

profile of v8, /device:TPU:1, one launch (start us, length us, event | category | flops | bytes accessed | tf_op | source)
XLA Modules:
  0.0 85.6 jit_solution(17643207894577294165)
XLA Ops:
  1.3 82.1 %shard_map.135 = (bf16[128,1536]{1,0:T(8,128)(2,1)}, bf16[128,1536]{1,0:T(8,128)(2,1)}, f32[12,1,1536]{2,1,0:T(1,128)}, f32[6,1,1536]{2,1,0:T(1,128)}, f32[6,1,3...) custom-call(s32[1]{0:T(128)S(6)} %copy.15.len_ref, bf16[128,1536]{1,0:T(8,128)(2,1)} %bitcast.12, ...), custom_call_target="tpu_custom_call" | custom-call | flops 2717908992 | bytes 12000000 | tf_op jit(solution)/shard_map/pallas_call | solution.py:920
  83.4 2.0 %shard_map.136 = (bf16[128,1536]{1,0:T(8,128)(2,1)}, bf16[128,1536]{1,0:T(8,128)(2,1)}, f32[12,1,1536]{2,1,0:T(1,128)}, f32[6,1,1536]{2,1,0:T(1,128)}, f32[6,1,3...) custom-call(bf16[128,1536]{1,0:T(8,128)(2,1)} %get-tuple-element.21.refs_0_, ...), custom_call_target="tpu_custom_call" | custom-call | tf_op jit(solution)/shard_map/pallas_call | solution.py:942
